TPU v7x, 128 devices: a whole 4x4x4 slice. The times are simulated.
128 devices in a mesh: seq: 16 (over y, x_hi, core), cp: 8 (over x_lo, z).
Axes of the slice: x: 4 (x_hi: 2, x_lo: 2; x = x_hi * 2 + x_lo), y: 4, z: 4, core: 2. Of those that a mesh axis runs over, the one named last changes fastest.
Arguments:
- hidden: bfloat16 [16, 1024, 1152], P('seq', 'cp'), may hold values from -6 to 6
- lengths: int32 [16], P('seq'), may hold values from 512 to 1024, as said below
- entry_gain: bfloat16 [1152], P(('seq', 'cp')), may hold values from 0.5 to 1.5
- query_weight: bfloat16 [1152, 1024], P(('seq', 'cp')), may hold values from -0.1875 to 0.1875
- key_weight: bfloat16 [1152, 256], P(('seq', 'cp')), may hold values from -0.1875 to 0.1875
- value_weight: bfloat16 [1152, 256], P(('seq', 'cp')), may hold values from -0.1875 to 0.1875
- query_gain: bfloat16 [256], P(('seq', 'cp')), may hold values from 0.5 to 1.5
- key_gain: bfloat16 [256], P(('seq', 'cp')), may hold values from 0.5 to 1.5
- output_weight: bfloat16 [1024, 1152], P(('seq', 'cp')), may hold values from -0.1875 to 0.1875
- mixer_gain: bfloat16 [1152], P(('seq', 'cp')), may hold values from 0.5 to 1.5
- feed_gain: bfloat16 [1152], P(('seq', 'cp')), may hold values from 0.5 to 1.5
- gate_weight: bfloat16 [1152, 6912], P(('seq', 'cp')), may hold values from -0.1875 to 0.1875
- up_weight: bfloat16 [1152, 6912], P(('seq', 'cp')), may hold values from -0.1875 to 0.1875
- down_weight: bfloat16 [6912, 1152], P(('seq', 'cp')), may hold values from -0.078125 to 0.078125
- closing_gain: bfloat16 [1152], P(('seq', 'cp')), may hold values from 0.5 to 1.5
- cotangent: bfloat16 [16, 1024, 1152], P('seq', 'cp'), may hold values from -6 to 6
Outputs:
- layer_output: bfloat16 [16, 1024, 1152], P('seq', 'cp')
- hidden_delta: float32 [16, 1024, 1152], P('seq', 'cp')
- entry_change: float32 [1152], P(('seq', 'cp'))
- query_delta: float32 [1152, 1024], P(('seq', 'cp'))
- key_delta: float32 [1152, 256], P(('seq', 'cp'))
- value_delta: float32 [1152, 256], P(('seq', 'cp'))
- query_change: float32 [256], P(('seq', 'cp'))
- key_change: float32 [256], P(('seq', 'cp'))
- output_delta: float32 [1024, 1152], P(('seq', 'cp'))
- mixer_change: float32 [1152], P(('seq', 'cp'))
- feed_change: float32 [1152], P(('seq', 'cp'))
- gate_delta: float32 [1152, 6912], P(('seq', 'cp'))
- upward_delta: float32 [1152, 6912], P(('seq', 'cp'))
- down_delta: float32 [6912, 1152], P(('seq', 'cp'))
- closing_change: float32 [1152], P(('seq', 'cp'))
Inputs may be any that keep to these rules, and one draw needn't show every extreme that they name: `lengths`: in every draw one sequence has all 1024 slots live.
All inputs are finite; a program needn't handle non-finite values.
Results may differ from a plain program's by a relative error of at most 0.033.
Values may be sent and summed in bfloat16 or wider, within the bound.
No kernel may reach another device: no remote copies, remote signals or barrier semaphores. Data moves between devices by JAX's collectives and lax.ppermute only.
A program may use at most 384 MiB of HBM per device.

v0:
```python
import jax
import jax.numpy as jnp
from jax import lax
from jax.sharding import PartitionSpec as P

epsilon = 1e-06


def normalize(values, scales):
    return values * lax.rsqrt(jnp.mean(values * values, axis=-1, keepdims=True) + epsilon) * scales


def folded_places(row_index, piece_rows, parts_cp):
    owner_index = row_index // (2 * piece_rows)
    inside = row_index % (2 * piece_rows)
    block_index = jnp.where(inside < piece_rows, owner_index, 2 * parts_cp - 1 - owner_index)
    return block_index * piece_rows + inside % piece_rows


def rotate(values, places):
    half_size = values.shape[-1] // 2
    frequency = 1000000.0 ** (-(jnp.arange(half_size, dtype=jnp.float32) * 2.0 / values.shape[-1]))
    angles = places.astype(jnp.float32)[:, None] * frequency[None, :]
    if values.ndim == 3:
        angles = angles[:, None, :]
    cosine = jnp.cos(angles)
    sine_part = jnp.sin(angles)
    front_half = values[..., :half_size]
    back_half = values[..., half_size:]
    return jnp.concatenate(
        [front_half * cosine - back_half * sine_part, back_half * cosine + front_half * sine_part],
        axis=-1,
    )


def query_piece(projected, scales, places, head_count):
    shaped = projected.reshape(projected.shape[0], head_count, -1)
    return rotate(normalize(shaped, scales), places) * scales.shape[0] ** (-0.5)


def key_piece(projected, scales, places):
    return rotate(normalize(projected, scales), places)


def gated(gate_out, up_out):
    return jax.nn.gelu(gate_out, approximate=True) * up_out


def row_term(left, right):
    return jnp.einsum("tr,te->re", left, right, preferred_element_type=jnp.float32)


def forward_pass(stream, live_length, places_own, places_all, mixer_set, feed_set, fetcher):
    (
        entry_gain,
        query_weight,
        key_weight,
        value_weight,
        query_gain,
        key_gain,
        output_weight,
        mixer_gain,
    ) = mixer_set
    feed_gain, gate_weight, up_weight, down_weight, closing_gain = feed_set
    count_rows = stream.shape[0]
    head_size = key_weight.shape[1]
    head_count = query_weight.shape[1] // head_size
    entry_in = normalize(stream, entry_gain.astype(jnp.float32)).astype(jnp.bfloat16)
    query_raw = jnp.dot(entry_in, query_weight, preferred_element_type=jnp.float32)
    key_raw = jnp.dot(entry_in, key_weight, preferred_element_type=jnp.float32)
    value_raw = jnp.dot(entry_in, value_weight, preferred_element_type=jnp.float32)
    query_low = query_piece(
        query_raw, query_gain.astype(jnp.float32), places_own, head_count
    ).astype(jnp.bfloat16)
    key_low = key_piece(key_raw, key_gain.astype(jnp.float32), places_own).astype(jnp.bfloat16)
    key_all, value_all = fetcher((key_low, value_raw.astype(jnp.bfloat16)))
    scores = jnp.einsum("qhd,kd->hqk", query_low, key_all, preferred_element_type=jnp.float32)
    allowed = (places_all[None, :] <= places_own[:, None]) & (places_all[None, :] < live_length)
    scores = jnp.where(allowed[None], scores, -1e30)
    soft_weights = jax.nn.softmax(scores, axis=-1)
    soft_low = soft_weights.astype(jnp.bfloat16)
    mixed_heads = jnp.einsum("hqk,kd->qhd", soft_low, value_all, preferred_element_type=jnp.float32)
    mixed_heads = mixed_heads.reshape(count_rows, head_count * head_size).astype(jnp.bfloat16)
    mixer_out = jnp.dot(mixed_heads, output_weight, preferred_element_type=jnp.float32)
    middle = stream + normalize(mixer_out, mixer_gain.astype(jnp.float32))
    feed_in = normalize(middle, feed_gain.astype(jnp.float32)).astype(jnp.bfloat16)
    gate_out = jnp.dot(feed_in, gate_weight, preferred_element_type=jnp.float32)
    up_out = jnp.dot(feed_in, up_weight, preferred_element_type=jnp.float32)
    product = gated(gate_out, up_out).astype(jnp.bfloat16)
    down_out = jnp.dot(product, down_weight, preferred_element_type=jnp.float32)
    result = middle + normalize(down_out, closing_gain.astype(jnp.float32))
    return {
        "stream": stream,
        "entry_in": entry_in,
        "query_raw": query_raw,
        "key_raw": key_raw,
        "query_low": query_low,
        "key_all": key_all,
        "value_all": value_all,
        "soft_weights": soft_weights,
        "soft_low": soft_low,
        "mixed_heads": mixed_heads,
        "mixer_out": mixer_out,
        "middle": middle,
        "feed_in": feed_in,
        "gate_out": gate_out,
        "up_out": up_out,
        "product": product,
        "down_out": down_out,
        "result": result,
    }


def backward_pass(state, upstream, places_own, mixer_set, feed_set, return_sums):
    (
        entry_gain,
        query_weight,
        key_weight,
        value_weight,
        query_gain,
        key_gain,
        output_weight,
        mixer_gain,
    ) = mixer_set
    feed_gain, gate_weight, up_weight, down_weight, closing_gain = feed_set
    count_rows = upstream.shape[0]
    head_size = key_weight.shape[1]
    head_count = query_weight.shape[1] // head_size
    _, closing_pull = jax.vjp(normalize, state["down_out"], closing_gain.astype(jnp.float32))
    down_grad, closing_change = closing_pull(upstream)
    down_grad = down_grad.astype(jnp.bfloat16)
    product_grad = jnp.einsum(
        "td,fd->tf", down_grad, down_weight, preferred_element_type=jnp.float32
    )
    _, gated_pull = jax.vjp(gated, state["gate_out"], state["up_out"])
    gate_grad, up_grad = gated_pull(product_grad)
    gate_grad = gate_grad.astype(jnp.bfloat16)
    up_grad = up_grad.astype(jnp.bfloat16)
    feed_in_grad = jnp.einsum(
        "tf,df->td", gate_grad, gate_weight, preferred_element_type=jnp.float32
    )
    feed_in_grad = feed_in_grad + jnp.einsum(
        "tf,df->td", up_grad, up_weight, preferred_element_type=jnp.float32
    )
    _, feed_pull = jax.vjp(normalize, state["middle"], feed_gain.astype(jnp.float32))
    middle_part, feed_change = feed_pull(feed_in_grad)
    middle_grad = upstream + middle_part
    _, mixer_pull = jax.vjp(normalize, state["mixer_out"], mixer_gain.astype(jnp.float32))
    mixer_out_grad, mixer_change = mixer_pull(middle_grad)
    mixer_out_grad = mixer_out_grad.astype(jnp.bfloat16)
    mixed_grad = jnp.einsum(
        "td,ed->te", mixer_out_grad, output_weight, preferred_element_type=jnp.float32
    )
    mixed_grad = mixed_grad.astype(jnp.bfloat16).reshape(count_rows, head_count, head_size)
    soft_weights = state["soft_weights"]
    value_dots = jnp.einsum(
        "qhd,kd->hqk", mixed_grad, state["value_all"], preferred_element_type=jnp.float32
    )
    score_grad = soft_weights * (
        value_dots - jnp.sum(soft_weights * value_dots, axis=-1, keepdims=True)
    )
    score_grad = score_grad.astype(jnp.bfloat16)
    key_term = jnp.einsum(
        "hqk,qhd->kd", score_grad, state["query_low"], preferred_element_type=jnp.float32
    )
    value_term = jnp.einsum(
        "hqk,qhd->kd", state["soft_low"], mixed_grad, preferred_element_type=jnp.float32
    )
    query_grad = jnp.einsum(
        "hqk,kd->qhd", score_grad, state["key_all"], preferred_element_type=jnp.float32
    )
    key_sum, value_sum = return_sums((key_term, value_term))
    _, query_pull = jax.vjp(
        lambda projected, scales: query_piece(projected, scales, places_own, head_count),
        state["query_raw"],
        query_gain.astype(jnp.float32),
    )
    query_raw_grad, query_change = query_pull(query_grad)
    _, key_pull = jax.vjp(
        lambda projected, scales: key_piece(projected, scales, places_own),
        state["key_raw"],
        key_gain.astype(jnp.float32),
    )
    key_raw_grad, key_change = key_pull(key_sum)
    query_raw_grad = query_raw_grad.astype(jnp.bfloat16)
    key_raw_grad = key_raw_grad.astype(jnp.bfloat16)
    value_raw_grad = value_sum.astype(jnp.bfloat16)
    entry_in_grad = jnp.einsum(
        "te,de->td", query_raw_grad, query_weight, preferred_element_type=jnp.float32
    )
    entry_in_grad = entry_in_grad + jnp.einsum(
        "te,de->td", key_raw_grad, key_weight, preferred_element_type=jnp.float32
    )
    entry_in_grad = entry_in_grad + jnp.einsum(
        "te,de->td", value_raw_grad, value_weight, preferred_element_type=jnp.float32
    )
    _, entry_pull = jax.vjp(normalize, state["stream"], entry_gain.astype(jnp.float32))
    stream_part, entry_change = entry_pull(entry_in_grad)
    hidden_delta = middle_grad + stream_part
    gain_changes = (
        entry_change,
        query_change,
        key_change,
        mixer_change,
        feed_change,
        closing_change,
    )
    projection_grads = jnp.concatenate([query_raw_grad, key_raw_grad, value_raw_grad], axis=1)
    gate_up_grads = jnp.concatenate([gate_grad, up_grad], axis=1)
    factors = (projection_grads, mixer_out_grad, gate_up_grads, down_grad)
    return (hidden_delta, gain_changes, factors)


def shards(
    hidden,
    lengths,
    entry_gain,
    query_weight,
    key_weight,
    value_weight,
    query_gain,
    key_gain,
    output_weight,
    mixer_gain,
    feed_gain,
    gate_weight,
    up_weight,
    down_weight,
    closing_gain,
    cotangent,
):
    count_rows = hidden.shape[1]
    parts_cp = lax.axis_size("cp")
    piece_rows = count_rows // 2
    places_all = folded_places(
        jnp.arange(count_rows * parts_cp, dtype=jnp.int32), piece_rows, parts_cp
    )
    places_own = folded_places(
        jnp.arange(count_rows, dtype=jnp.int32) + lax.axis_index("cp") * count_rows,
        piece_rows,
        parts_cp,
    )
    live_length = lengths[0]
    stream = hidden[0].astype(jnp.float32)
    mixer_set = (
        lax.all_gather(entry_gain, ("seq", "cp"), axis=0, tiled=True),
        lax.all_gather(query_weight, ("seq", "cp"), axis=0, tiled=True),
        lax.all_gather(key_weight, ("seq", "cp"), axis=0, tiled=True),
        lax.all_gather(value_weight, ("seq", "cp"), axis=0, tiled=True),
        lax.all_gather(query_gain, ("seq", "cp"), axis=0, tiled=True),
        lax.all_gather(key_gain, ("seq", "cp"), axis=0, tiled=True),
        lax.all_gather(output_weight, ("seq", "cp"), axis=0, tiled=True),
        lax.all_gather(mixer_gain, ("seq", "cp"), axis=0, tiled=True),
    )
    feed_set = (
        lax.all_gather(feed_gain, ("seq", "cp"), axis=0, tiled=True),
        lax.all_gather(gate_weight, ("seq", "cp"), axis=0, tiled=True),
        lax.all_gather(up_weight, ("seq", "cp"), axis=0, tiled=True),
        lax.all_gather(down_weight, ("seq", "cp"), axis=0, tiled=True),
        lax.all_gather(closing_gain, ("seq", "cp"), axis=0, tiled=True),
    )
    state = forward_pass(
        stream,
        live_length,
        places_own,
        places_all,
        mixer_set,
        feed_set,
        lambda couple: (
            lax.all_gather(couple[0], "cp", axis=0, tiled=True),
            lax.all_gather(couple[1], "cp", axis=0, tiled=True),
        ),
    )
    layer_output = state["result"].astype(jnp.bfloat16)[None]
    mixer_set = (
        lax.all_gather(entry_gain, ("seq", "cp"), axis=0, tiled=True),
        lax.all_gather(query_weight, ("seq", "cp"), axis=0, tiled=True),
        lax.all_gather(key_weight, ("seq", "cp"), axis=0, tiled=True),
        lax.all_gather(value_weight, ("seq", "cp"), axis=0, tiled=True),
        lax.all_gather(query_gain, ("seq", "cp"), axis=0, tiled=True),
        lax.all_gather(key_gain, ("seq", "cp"), axis=0, tiled=True),
        lax.all_gather(output_weight, ("seq", "cp"), axis=0, tiled=True),
        lax.all_gather(mixer_gain, ("seq", "cp"), axis=0, tiled=True),
    )
    feed_set = (
        lax.all_gather(feed_gain, ("seq", "cp"), axis=0, tiled=True),
        lax.all_gather(gate_weight, ("seq", "cp"), axis=0, tiled=True),
        lax.all_gather(up_weight, ("seq", "cp"), axis=0, tiled=True),
        lax.all_gather(down_weight, ("seq", "cp"), axis=0, tiled=True),
        lax.all_gather(closing_gain, ("seq", "cp"), axis=0, tiled=True),
    )
    state = forward_pass(
        stream,
        live_length,
        places_own,
        places_all,
        mixer_set,
        feed_set,
        lambda couple: (
            lax.all_gather(couple[0], "cp", axis=0, tiled=True),
            lax.all_gather(couple[1], "cp", axis=0, tiled=True),
        ),
    )
    hidden_delta, gain_changes, factors = backward_pass(
        state,
        cotangent[0].astype(jnp.float32),
        places_own,
        mixer_set,
        feed_set,
        lambda couple: (
            lax.psum_scatter(
                couple[0].astype(jnp.bfloat16), "cp", scatter_dimension=0, tiled=True
            ).astype(jnp.float32),
            lax.psum_scatter(
                couple[1].astype(jnp.bfloat16), "cp", scatter_dimension=0, tiled=True
            ).astype(jnp.float32),
        ),
    )
    entry_change, query_change, key_change, mixer_change, feed_change, closing_change = gain_changes
    projection_grads, mixer_out_grad, gate_up_grads, down_grad = factors
    gain_shares = (
        lax.psum_scatter(entry_change, ("seq", "cp"), scatter_dimension=0, tiled=True),
        lax.psum_scatter(query_change, ("seq", "cp"), scatter_dimension=0, tiled=True),
        lax.psum_scatter(key_change, ("seq", "cp"), scatter_dimension=0, tiled=True),
        lax.psum_scatter(mixer_change, ("seq", "cp"), scatter_dimension=0, tiled=True),
        lax.psum_scatter(feed_change, ("seq", "cp"), scatter_dimension=0, tiled=True),
        lax.psum_scatter(closing_change, ("seq", "cp"), scatter_dimension=0, tiled=True),
    )
    query_width = query_weight.shape[1]
    key_width = key_weight.shape[1]
    feed_width = gate_weight.shape[1]
    projection_share = lax.psum_scatter(
        row_term(state["entry_in"], projection_grads),
        ("seq", "cp"),
        scatter_dimension=0,
        tiled=True,
    )
    output_share = lax.psum_scatter(
        row_term(state["mixed_heads"], mixer_out_grad),
        ("seq", "cp"),
        scatter_dimension=0,
        tiled=True,
    )
    gate_up_share = lax.psum_scatter(
        row_term(state["feed_in"], gate_up_grads), ("seq", "cp"), scatter_dimension=0, tiled=True
    )
    down_share = lax.psum_scatter(
        row_term(state["product"], down_grad), ("seq", "cp"), scatter_dimension=0, tiled=True
    )
    query_delta = projection_share[:, :query_width]
    key_delta = projection_share[:, query_width : query_width + key_width]
    value_delta = projection_share[:, query_width + key_width :]
    gate_delta = gate_up_share[:, :feed_width]
    upward_delta = gate_up_share[:, feed_width:]
    return (
        layer_output,
        hidden_delta[None],
        gain_shares[0],
        query_delta,
        key_delta,
        value_delta,
        gain_shares[1],
        gain_shares[2],
        output_share,
        gain_shares[3],
        gain_shares[4],
        gate_delta,
        upward_delta,
        down_share,
        gain_shares[5],
    )


def solution(mesh):
    placed = (
        P("seq", "cp", None),
        P("seq"),
        P(("seq", "cp")),
        P(("seq", "cp"), None),
        P(("seq", "cp"), None),
        P(("seq", "cp"), None),
        P(("seq", "cp")),
        P(("seq", "cp")),
        P(("seq", "cp"), None),
        P(("seq", "cp")),
        P(("seq", "cp")),
        P(("seq", "cp"), None),
        P(("seq", "cp"), None),
        P(("seq", "cp"), None),
        P(("seq", "cp")),
        P("seq", "cp", None),
    )
    return jax.shard_map(
        shards,
        mesh=mesh,
        in_specs=placed,
        out_specs=(
            P("seq", "cp", None),
            P("seq", "cp", None),
            P(("seq", "cp")),
            P(("seq", "cp"), None),
            P(("seq", "cp"), None),
            P(("seq", "cp"), None),
            P(("seq", "cp")),
            P(("seq", "cp")),
            P(("seq", "cp"), None),
            P(("seq", "cp")),
            P(("seq", "cp")),
            P(("seq", "cp"), None),
            P(("seq", "cp"), None),
            P(("seq", "cp"), None),
            P(("seq", "cp")),
        ),
        check_vma=False,
    )
```

profile of v0, /device:TPU:8, one launch (start us, length us, event | category | flops | bytes accessed | tf_op | source)
XLA Modules:
  0.0 2744.6 jit_solution(17564390498462466994)
XLA Ops:
  16.4 67.2 %all-reduce.23 = (bf16[1152]{0:T(1024)(128)(2,1)S(1)}, bf16[256]{0:T(256)(128)(2,1)S(1)}, bf16[256]{0:T(256)(128)(2,1)S(1)}, bf16[1152]{0:T(1024)(128)(2,1)S(1)}...) all-reduce(bf16[1152]{0:T(1024)(128)(2,1)S(1)} %dynamic-update-slic, ...), channel_id=1, replica_groups=mesh['seq'=16,'cp'=8] {'seq','cp'}, use_global_device_ids=true, to_apply=%add.4 | all-reduce | flops 5120 | bytes 20480
  84.8 280.3 %all-gather.1 = bf16[128,9,256]{2,1,0:T(8,128)(2,1)S(1)} all-gather(bf16[1,9,256]{2,1,0:T(8,128)(2,1)} %bitcast.183), channel_id=1, replica_groups=mesh['seq'=16,'cp'=8] {'seq','cp'}, dimensions={0}, use_global_device_ids=true | all-gather | bytes 594432 | tf_op jit(solution)/shard_map/all_gather | solution.py:248
  365.4 278.7 %all-gather = bf16[128,9,256]{2,1,0:T(8,128)(2,1)S(1)} all-gather(bf16[1,9,256]{2,1,0:T(8,128)(2,1)} %bitcast.184), channel_id=1, replica_groups=mesh['seq'=16,'cp'=8] {'seq','cp'}, dimensions={0}, use_global_device_ids=true | all-gather | bytes 594432 | tf_op jit(solution)/shard_map/all_gather | solution.py:249
  646.4 29.0 %all_gather.65 = bf16[1024,256]{1,0:T(8,128)(2,1)S(1)} all-gather(bf16[128,256]{1,0:T(8,128)(2,1)S(1)} %pad_maximum_fusion), channel_id=1, replica_groups=mesh['seq'=16,'cp'=8] {'cp'}, dimensions={0}, use_global_device_ids=true | all-gather | bytes 589824 | tf_op jit(solution)/shard_map/all_gather | solution.py:270
  675.7 31.0 %all_gather.62 = bf16[1024,256]{1,0:T(8,128)(2,1)} all-gather(bf16[128,256]{1,0:T(8,128)(2,1)S(1)} %convolution_convert_fusion.2), channel_id=1, replica_groups=mesh['seq'=16,'cp'=8] {'cp'}, dimensions={0}, use_global_device_ids=true | all-gather | bytes 589824 | tf_op jit(solution)/shard_map/all_gather | solution.py:271
  706.8 4.2 reshape.388
  711.0 2.8 copy.50
  713.8 2.7 multiply_reduce_fusion.9
  717.6 2.1 fusion.140
  721.0 2.4 multiply_reduce_fusion.6
  724.8 241.6 %all-gather.16.cloned.1.call-done = bf16[128,9,6912]{2,1,0:T(8,128)(2,1)} async-done(((bf16[1,9,6912]{2,1,0:T(8,128)(2,1)}), bf16[128,9,6912]{2,1,0:T(8,128)(2,1)}) %all-gather.16.cloned.1.call-update) | async-done | bytes 15925264 | tf_op jit(solution)/shard_map/all_gather | solution.py:257
  966.4 22.4 reshape.390
  988.8 322.8 %all-gather.18.cloned.1.call-done = bf16[128,9,6912]{2,1,0:T(8,128)(2,1)} async-done(((bf16[1,9,6912]{2,1,0:T(8,128)(2,1)}), bf16[128,9,6912]{2,1,0:T(8,128)(2,1)}) %all-gather.18.cloned.1.call-update) | async-done | bytes 15925264 | tf_op jit(solution)/shard_map/all_gather | solution.py:258
  1311.6 22.4 reshape.392
  1334.0 8.2 fusion.145
  1342.3 1.8 copy-done.3
  1345.5 4.7 multiply_convert_fusion.1
  1350.2 290.1 %all-gather.20.cloned.1.call-done = bf16[128,54,1152]{2,1,0:T(8,128)(2,1)} async-done(((bf16[1,54,1152]{2,1,0:T(8,128)(2,1)}), bf16[128,54,1152]{2,1,0:T(8,128)(2,1)}) %all-gather.20.cloned.1.call-update) | async-done | bytes 15925264 | tf_op jit(solution)/shard_map/all_gather | solution.py:259
  1640.3 18.7 reshape.394
  1659.0 8.2 multiply_reduce_fusion.4
  1669.1 10.4 multiply_convert_fusion
  1679.5 11.2 fusion.146
  1690.7 12.6 multiply_reduce_fusion
  1703.4 2.2 multiply_reduce_fusion.1
  1712.6 24.9 fusion.9
  1740.4 3.4 fusion.18
  1744.0 2.9 fusion.148
  1746.9 30.0 %reduce-scatter.5.cloned.1.call-done = bf16[128,256]{1,0:T(8,128)(2,1)} async-done(((bf16[1024,256]{1,0:T(8,128)(2,1)}), bf16[128,256]{1,0:T(8,128)(2,1)}) %reduce-scatter.5.cloned.1.call-update) | async-done | bytes 65552 | tf_op jit(solution)/shard_map/reduce_scatter | solution.py:311
  1778.5 37.5 %reduce-scatter.7.cloned.1.call-done = bf16[128,256]{1,0:T(8,128)(2,1)} async-done(((bf16[1024,256]{1,0:T(8,128)(2,1)}), bf16[128,256]{1,0:T(8,128)(2,1)}) %reduce-scatter.7.cloned.1.call-update) | async-done | bytes 65552 | tf_op jit(solution)/shard_map/reduce_scatter | solution.py:314
  1817.0 4.0 fusion.53
  1821.9 14.0 fusion.149
  1835.9 525.7 %fusion = f32[64,1152]{1,0:T(8,128)S(1)} fusion(f32[6912,1152]{1,0:T(8,128)} %fusion.149), kind=kCustom, calls=%all-reduce-scatter | all-reduce-scatter fusion | flops 9437185 | bytes 32145408
  2361.7 1.9 collective-permute-start.18
  2363.6 4.2 collective-permute-start.17
  2367.8 3.0 collective-permute-start.16
  2370.8 2.6 collective-permute-start.15
  2373.4 5.6 collective-permute-start.19
  2379.0 27.4 collective-permute-done.19
  2406.4 7.2 collective-permute-start.14
  2413.7 1.9 collective-permute-start.13
  2415.6 1.9 collective-permute-start.12
  2417.6 1.9 collective-permute-start.11
  2419.5 9.1 collective-permute-start.10
  2428.6 1.9 collective-permute-start.9
  2430.6 2.8 collective-permute-done.13
  2433.4 1.9 collective-permute-start.8
  2435.3 4.1 collective-permute-done.12
  2439.4 1.9 collective-permute-start.7
  2441.3 19.9 collective-permute-done.11
  2461.3 1.9 collective-permute-start.6
  2463.2 1.9 collective-permute-start.5
  2465.2 3.6 collective-permute-done.9
  2468.9 1.9 collective-permute-start.4
  2470.8 13.5 collective-permute-done.8
  2484.2 1.9 collective-permute-start.3
  2486.2 1.9 collective-permute-start.2
  2488.1 1.9 collective-permute-start.1
  2490.0 4.3 collective-permute-start
  2496.1 7.1 collective-permute-done.2
  2504.6 3.2 collective-permute-done
  2507.8 36.6 %concatenate.19 = f32[1334,1152]{1,0:T(8,128)} concatenate(f32[54,1152]{1,0:T(8,128)} %collective-permute-done.19, f32[64,1152]{1,0:T(8,128)} %copy-done.36, f32[64,1152]{1,0:T(8,128)} %copy-done.37, f32[64,1152]{1,0:T(8,128)} %copy-done.38, f32[64,1152]{1,0:T(8,128)} %copy-done.39, f32[64,1152]{1,0:T(8,128)} %copy-done.40, f32[64,1152]{1,0:T(8,128)} %copy-done.41, ...), dimensions={0} | concatenate | bytes 12294144
  2547.1 71.9 %all-reduce.21 = (f32[1152]{0:T(1024)S(1)}, f32[256]{0:T(256)S(1)}, f32[256]{0:T(256)S(1)}, f32[1152]{0:T(1024)S(1)}, f32[1152]{0:T(1024)S(1)}, /*index=5*/f32[1152]{0:T(1024)S(1)}) all-reduce(f32[1152]{0:T(1024)S(1)} %get-tuple-element.23, f32[256]{0:T(256)S(1)} %copy-done.78, ...), channel_id=4, replica_groups=mesh['seq'=16,'cp'=8] {'seq','cp'}, use_global_device_ids=true, to_apply=%region_18.19.clone | all-reduce | flops 5120 | bytes 40960
  2623.5 107.2 %all-reduce.26.cloned.1.call-done = (f32[1152,1536]{1,0:T(8,128)}, f32[1024,1152]{1,0:T(8,128)}, f32[1152,13824]{1,0:T(8,128)}) async-done(((f32[1152,1536]{1,0:T(8,128)}, f32[1024,1152]{1,0:T(8,128)}, f32[1152,13824]{1,0:T(8,128)}), (f32[1152,1536]{1,0:T(8,128)}, f32[1024,1152]{1,0:T(8,128)}, f32[1152,13824]{1,0:T(8,128)})) %all-reduce.26.cloned.1.call-update) | async-done | bytes 75497488
  2735.2 2.3 fusion.138
  (299 shorter events, 47.3 us)
Async XLA Ops:
  7.2 637.3 %copy-start.5 = (bf16[1,128,1152]{2,1,0:T(8,128)(2,1)S(1)}, bf16[1,128,1152]{2,1,0:T(8,128)(2,1)}, u32[]{:S(2)}) copy-start(bf16[1,128,1152]{2,1,0:T(8,128)(2,1)} %param.16) | copy-start | bytes 884740
  7.2 699.6 %all-gather.14.cloned.1.call-start = ((), (), s32[]{:S(2)}) async-start(), calls=%async_computation.5 | async-start | bytes 4227072 | tf_op jit(solution)/shard_map/all_gather | solution.py:247
  7.9 713.0 %all-gather.12.cloned.1.call-start = ((), (), s32[]{:S(2)}) async-start(), calls=%async_computation.2 | async-start | bytes 2377728 | tf_op jit(solution)/shard_map/all_gather | solution.py:252
  8.7 957.7 %all-gather.16.cloned.1.call-start = ((), (), s32[]{:S(2)}) async-start(), calls=%async_computation.6 | async-start | bytes 28532736 | tf_op jit(solution)/shard_map/all_gather | solution.py:257
  9.4 1302.2 %all-gather.18.cloned.1.call-start = ((), (), s32[]{:S(2)}) async-start(), calls=%async_computation.7 | async-start | bytes 28532736 | tf_op jit(solution)/shard_map/all_gather | solution.py:258
  10.0 1630.3 %all-gather.20.cloned.1.call-start = ((), (), s32[]{:S(2)}) async-start(), calls=%async_computation.8 | async-start | bytes 16644096 | tf_op jit(solution)/shard_map/all_gather | solution.py:259
  10.6 1766.3 %reduce-scatter.5.cloned.1.call-start = ((), (), s32[]{:S(2)}) async-start(), calls=%async_computation.3 | async-start | bytes 589824 | tf_op jit(solution)/shard_map/reduce_scatter | solution.py:311
  83.6 562.1 %copy-start.69 = (f32[256]{0:T(256)}, f32[256]{0:T(256)S(1)}, u32[]{:S(2)}) copy-start(f32[256]{0:T(256)S(1)} %convert_element_type.143) | copy-start | bytes 3076
  83.6 633.0 %copy-start.71 = (f32[256]{0:T(256)}, f32[256]{0:T(256)S(1)}, u32[]{:S(2)}) copy-start(f32[256]{0:T(256)S(1)} %convert_element_type.148) | copy-start | bytes 3076
  365.4 341.4 %copy-start.16 = (bf16[1152,256]{1,0:T(8,128)(2,1)}, bf16[1152,256]{1,0:T(8,128)(2,1)S(1)}, u32[]{:S(2)}) copy-start(bf16[1152,256]{1,0:T(8,128)(2,1)S(1)} %reshape.386) | copy-start | bytes 1769476
  644.3 62.4 %copy-start.18 = (bf16[1152,256]{1,0:T(8,128)(2,1)}, bf16[1152,256]{1,0:T(8,128)(2,1)S(1)}, u32[]{:S(2)}) copy-start(bf16[1152,256]{1,0:T(8,128)(2,1)S(1)} %reshape.384) | copy-start | bytes 1769476
  644.3 66.6 %copy-start.82 = (f32[128]{0:T(128)}, f32[128]{0:T(128)S(1)}, u32[]{:S(2)}) copy-start(f32[128]{0:T(128)S(1)} %fusion.112) | copy-start | bytes 1540
  644.4 66.6 %copy-start.84 = (f32[128]{0:T(128)}, f32[128]{0:T(128)S(1)}, u32[]{:S(2)}) copy-start(f32[128]{0:T(128)S(1)} %negate_power_fusion) | copy-start | bytes 1540
  644.6 69.2 %copy-start.67 = (f32[128]{0:T(128)}, f32[128]{0:T(128)S(1)}, u32[]{:S(2)}) copy-start(f32[128]{0:T(128)S(1)} %fusion.104) | copy-start | bytes 1540
  645.1 61.6 %copy-start.24 = (f32[128,256]{1,0:T(8,128)}, f32[128,256]{1,0:T(8,128)S(1)}, u32[]{:S(2)}) copy-start(f32[128,256]{1,0:T(8,128)S(1)} %get-tuple-element.66) | copy-start | bytes 393220
  645.6 65.4 %copy-start.74 = (f32[128]{0:T(128)}, f32[128]{0:T(128)S(1)}, u32[]{:S(2)}) copy-start(f32[128]{0:T(128)S(1)} %fusion.105) | copy-start | bytes 1540
  646.0 71.4 %copy-start.30 = (f32[128,128]{1,0:T(8,128)}, f32[128,128]{1,0:T(8,128)S(1)}, u32[]{:S(2)}) copy-start(f32[128,128]{1,0:T(8,128)S(1)} %get-tuple-element.61) | copy-start | bytes 196612
  646.0 71.4 %copy-start.32 = (f32[128,128]{1,0:T(8,128)}, f32[128,128]{1,0:T(8,128)S(1)}, u32[]{:S(2)}) copy-start(f32[128,128]{1,0:T(8,128)S(1)} %get-tuple-element.62) | copy-start | bytes 196612
  646.4 73.3 %copy-start.58 = (pred[128,1024]{0,1:T(8,128)(4,1)}, pred[128,1024]{0,1:T(8,128)(4,1)S(1)}, u32[]{:S(2)}) copy-start(pred[128,1024]{0,1:T(8,128)(4,1)S(1)} %compare_and_fusion) | copy-start | bytes 393220
  675.4 44.3 %copy-start.22 = (bf16[1024,256]{1,0:T(8,128)(2,1)}, bf16[1024,256]{1,0:T(8,128)(2,1)S(1)}, u32[]{:S(2)}) copy-start(bf16[1024,256]{1,0:T(8,128)(2,1)S(1)} %all_gather.65) | copy-start | bytes 1572868
  720.9 267.9 %copy-start.28 = (bf16[256,4,128]{2,0,1:T(8,128)(2,1)}, bf16[256,4,128]{2,0,1:T(8,128)(2,1)S(1)}, u32[]{:S(2)}) copy-start(bf16[256,4,128]{2,0,1:T(8,128)(2,1)S(1)} %convolution_convert_fusion.1) | copy-start | bytes 786436
  724.6 264.2 %copy-start.76 = (f32[128]{0:T(128)}, f32[128]{0:T(128)S(1)}, u32[]{:S(2)}) copy-start(f32[128]{0:T(128)S(1)} %fusion.107) | copy-start | bytes 1540
  1737.5 78.5 %reduce-scatter.7.cloned.1.call-start = ((), (), s32[]{:S(2)}) async-start(), calls=%async_computation.4 | async-start | bytes 589824 | tf_op jit(solution)/shard_map/reduce_scatter | solution.py:314
  1743.8 33.9 %copy-start.83 = (f32[128]{0:T(128)S(1)}, f32[128]{0:T(128)}, u32[]{:S(2)}) copy-start(f32[128]{0:T(128)} %copy-done.82) | copy-start | bytes 1540
  1743.8 33.9 %copy-start.85 = (f32[128]{0:T(128)S(1)}, f32[128]{0:T(128)}, u32[]{:S(2)}) copy-start(f32[128]{0:T(128)} %copy-done.84) | copy-start | bytes 1540
  1743.8 34.2 %copy-start.25 = (f32[128,256]{1,0:T(8,128)S(1)}, f32[128,256]{1,0:T(8,128)}, u32[]{:S(2)}) copy-start(f32[128,256]{1,0:T(8,128)} %copy-done.24) | copy-start | bytes 393220
  1743.8 34.2 %copy-start.70 = (f32[256]{0:T(256)S(1)}, f32[256]{0:T(256)}, u32[]{:S(2)}) copy-start(f32[256]{0:T(256)} %copy-done.69) | copy-start | bytes 3076
  1743.8 34.2 %copy-start.75 = (f32[128]{0:T(128)S(1)}, f32[128]{0:T(128)}, u32[]{:S(2)}) copy-start(f32[128]{0:T(128)} %copy-done.74) | copy-start | bytes 1540
  1743.8 34.4 %copy-start.93 = (f32[128]{0:T(128)S(1)}, f32[128]{0:T(128)}, u32[]{:S(2)}) copy-start(f32[128]{0:T(128)} %copy-done.92) | copy-start | bytes 1540
  1743.8 73.1 %copy-start.68 = (f32[128]{0:T(128)S(1)}, f32[128]{0:T(128)}, u32[]{:S(2)}) copy-start(f32[128]{0:T(128)} %copy-done.67) | copy-start | bytes 1540
  1743.9 986.9 %all-reduce.26.cloned.1.call-start = ((), (), s32[]{:S(2)}) async-start(), calls=%async_computation.9 | async-start | bytes 150994944
  1835.9 658.4 %copy-start.2 = (bf16[1152,1024]{1,0:T(8,128)(2,1)S(1)}, bf16[1152,1024]{1,0:T(8,128)(2,1)}, u32[]{:S(2)}) copy-start(bf16[1152,1024]{1,0:T(8,128)(2,1)} %copy-done.1) | copy-start | bytes 7077892
  2361.7 52.0 %collective-permute-start.18 = (f32[64,1152]{1,0:T(8,128)S(1)}, f32[64,1152]{1,0:T(8,128)S(1)}, u32[]{:S(2)}, u32[]{:S(2)}) collective-permute-start(f32[64,1152]{1,0:T(8,128)S(1)} %fusion), channel_id=1, source_target_pairs={{0,19},{1,20},{2,21},{3,22},{4,23},{5,24},{6,25},{7,26},{8,27},{9,... | collective-permute-start | bytes 884744
  2363.6 52.0 %collective-permute-start.17 = (f32[64,1152]{1,0:T(8,128)S(1)}, f32[64,1152]{1,0:T(8,128)S(1)}, u32[]{:S(2)}, u32[]{:S(2)}) collective-permute-start(f32[64,1152]{1,0:T(8,128)S(1)} %fusion), channel_id=1, source_target_pairs={{0,18},{1,19},{2,20},{3,21},{4,22},{5,23},{6,24},{7,25},{8,26},{9,... | collective-permute-start | bytes 884744
  2367.8 49.8 %collective-permute-start.16 = (f32[64,1152]{1,0:T(8,128)S(1)}, f32[64,1152]{1,0:T(8,128)S(1)}, u32[]{:S(2)}, u32[]{:S(2)}) collective-permute-start(f32[64,1152]{1,0:T(8,128)S(1)} %fusion), channel_id=1, source_target_pairs={{0,17},{1,18},{2,19},{3,20},{4,21},{5,22},{6,23},{7,24},{8,25},{9,... | collective-permute-start | bytes 884744
  2370.8 48.7 %collective-permute-start.15 = (f32[64,1152]{1,0:T(8,128)S(1)}, f32[64,1152]{1,0:T(8,128)S(1)}, u32[]{:S(2)}, u32[]{:S(2)}) collective-permute-start(f32[64,1152]{1,0:T(8,128)S(1)} %fusion), channel_id=1, source_target_pairs={{0,16},{1,17},{2,18},{3,19},{4,20},{5,21},{6,22},{7,23},{8,24},{9,... | collective-permute-start | bytes 884744
  2373.4 33.0 %collective-permute-start.19 = (f32[54,1152]{1,0:T(8,128)S(1)}, f32[54,1152]{1,0:T(8,128)}, u32[]{:S(2)}, u32[]{:S(2)}) collective-permute-start(f32[54,1152]{1,0:T(8,128)S(1)} %slice.44), channel_id=1, source_target_pairs={{0,20},{1,21},{2,22},{3,23},{4,24},{5,25},{6,26},{7,27},{8,28},{9,... | collective-permute-start | bytes 746504
  2406.4 22.2 collective-permute-start.14
  2413.7 49.5 %copy-start.36 = (f32[64,1152]{1,0:T(8,128)}, f32[64,1152]{1,0:T(8,128)S(1)}, u32[]{:S(2)}) copy-start(f32[64,1152]{1,0:T(8,128)S(1)} %collective-permute-done.18) | copy-start | bytes 884740
  2413.7 19.7 collective-permute-start.13
  2415.6 49.5 %copy-start.37 = (f32[64,1152]{1,0:T(8,128)}, f32[64,1152]{1,0:T(8,128)S(1)}, u32[]{:S(2)}) copy-start(f32[64,1152]{1,0:T(8,128)S(1)} %collective-permute-done.17) | copy-start | bytes 884740
  2415.6 23.8 collective-permute-start.12
  2417.6 47.6 %copy-start.38 = (f32[64,1152]{1,0:T(8,128)}, f32[64,1152]{1,0:T(8,128)S(1)}, u32[]{:S(2)}) copy-start(f32[64,1152]{1,0:T(8,128)S(1)} %collective-permute-done.16) | copy-start | bytes 884740
  2417.6 43.7 %collective-permute-start.11 = (f32[64,1152]{1,0:T(8,128)S(1)}, f32[64,1152]{1,0:T(8,128)S(1)}, u32[]{:S(2)}, u32[]{:S(2)}) collective-permute-start(f32[64,1152]{1,0:T(8,128)S(1)} %fusion), channel_id=1, source_target_pairs={{0,12},{1,13},{2,14},{3,15},{4,16},{5,17},{6,18},{7,19},{8,20},{9,... | collective-permute-start | bytes 884744
  2419.5 45.6 %copy-start.39 = (f32[64,1152]{1,0:T(8,128)}, f32[64,1152]{1,0:T(8,128)S(1)}, u32[]{:S(2)}) copy-start(f32[64,1152]{1,0:T(8,128)S(1)} %collective-permute-done.15) | copy-start | bytes 884740
  2419.5 43.6 %collective-permute-start.10 = (f32[64,1152]{1,0:T(8,128)S(1)}, f32[64,1152]{1,0:T(8,128)S(1)}, u32[]{:S(2)}, u32[]{:S(2)}) collective-permute-start(f32[64,1152]{1,0:T(8,128)S(1)} %fusion), channel_id=1, source_target_pairs={{0,11},{1,12},{2,13},{3,14},{4,15},{5,16},{6,17},{7,18},{8,19},{9,... | collective-permute-start | bytes 884744
  2428.6 36.5 %copy-start.40 = (f32[64,1152]{1,0:T(8,128)}, f32[64,1152]{1,0:T(8,128)S(1)}, u32[]{:S(2)}) copy-start(f32[64,1152]{1,0:T(8,128)S(1)} %collective-permute-done.14) | copy-start | bytes 884740
  2428.6 40.2 %collective-permute-start.9 = (f32[64,1152]{1,0:T(8,128)S(1)}, f32[64,1152]{1,0:T(8,128)}, u32[]{:S(2)}, u32[]{:S(2)}) collective-permute-start(f32[64,1152]{1,0:T(8,128)S(1)} %fusion), channel_id=1, source_target_pairs={{0,10},{1,11},{2,12},{3,13},{4,14},{5,15},{6,16},{7,17},{8,18},{9,... | collective-permute-start | bytes 884744
  2433.4 31.8 %copy-start.41 = (f32[64,1152]{1,0:T(8,128)}, f32[64,1152]{1,0:T(8,128)S(1)}, u32[]{:S(2)}) copy-start(f32[64,1152]{1,0:T(8,128)S(1)} %collective-permute-done.13) | copy-start | bytes 884740
  2433.4 50.9 %collective-permute-start.8 = (f32[64,1152]{1,0:T(8,128)S(1)}, f32[64,1152]{1,0:T(8,128)}, u32[]{:S(2)}, u32[]{:S(2)}) collective-permute-start(f32[64,1152]{1,0:T(8,128)S(1)} %fusion), channel_id=1, source_target_pairs={{0,9},{1,10},{2,11},{3,12},{4,13},{5,14},{6,15},{7,16},{8,17},{9,1... | collective-permute-start | bytes 884744
  2439.4 46.8 %collective-permute-start.7 = (f32[64,1152]{1,0:T(8,128)S(1)}, f32[64,1152]{1,0:T(8,128)}, u32[]{:S(2)}, u32[]{:S(2)}) collective-permute-start(f32[64,1152]{1,0:T(8,128)S(1)} %fusion), channel_id=1, source_target_pairs={{0,8},{1,9},{2,10},{3,11},{4,12},{5,13},{6,14},{7,15},{8,16},{9,17... | collective-permute-start | bytes 884744
  2461.3 26.8 collective-permute-start.6
  2463.2 26.8 collective-permute-start.5
  2468.9 27.2 collective-permute-start.4
  2484.2 11.8 collective-permute-start.3
  2486.2 17.1 collective-permute-start.2
  2488.1 15.6 collective-permute-start.1
  2490.0 17.8 collective-permute-start
  2496.0 50.2 %copy-start.17 = (bf16[1152,256]{1,0:T(8,128)(2,1)S(1)}, bf16[1152,256]{1,0:T(8,128)(2,1)}, u32[]{:S(2)}) copy-start(bf16[1152,256]{1,0:T(8,128)(2,1)} %copy-done.16) | copy-start | bytes 1769476
  2496.0 50.2 %copy-start.20 = (f32[128,1152]{1,0:T(8,128)S(1)}, f32[128,1152]{1,0:T(8,128)}, u32[]{:S(2)}) copy-start(f32[128,1152]{1,0:T(8,128)} %fusion.147) | copy-start | bytes 1769476
  2496.1 50.5 %copy-start.19 = (bf16[1152,256]{1,0:T(8,128)(2,1)S(1)}, bf16[1152,256]{1,0:T(8,128)(2,1)}, u32[]{:S(2)}) copy-start(bf16[1152,256]{1,0:T(8,128)(2,1)} %copy-done.18) | copy-start | bytes 1769476
  2496.1 50.6 %copy-start.51 = (bf16[128,256]{1,0:T(8,128)(2,1)S(1)}, bf16[128,256]{1,0:T(8,128)(2,1)}, u32[]{:S(2)}) copy-start(bf16[128,256]{1,0:T(8,128)(2,1)} %reduce-scatter.7.cloned.1.call-done) | copy-start | bytes 196612
  2544.5 78.0 %copy-start.89 = (f32[128]{0:T(128)S(1)}, f32[128]{0:T(128)}, u32[]{:S(2)}) copy-start(f32[128]{0:T(128)} %copy-done.88) | copy-start | bytes 1540
  2544.5 78.0 %copy-start.11 = (f32[128,1152]{1,0:T(8,128)S(1)}, f32[128,1152]{1,0:T(8,128)}, u32[]{:S(2)}) copy-start(f32[128,1152]{1,0:T(8,128)} %copy-done.10) | copy-start | bytes 1769476
  (58 other events, 381.7 us)
Sparse Core Ops, SparseCore 0:
  9.7 307.6 all-gather.13
  319.1 302.0 all-gather.11
  622.9 343.4 all-gather.15
  967.9 343.6 all-gather.17
  1313.2 327.0 all-gather.19
  1737.7 39.1 reduce-scatter.4
  1779.3 36.6 reduce-scatter.6
  1822.4 908.3 all-reduce.25
where the time goes:
time: 2760 us; the launch traced here: 2740 us
  blocking collectives  1280 us (46%)
  waiting for transfers between devices  1110 us (40%)
  local copies, waits for them, and re-layouts  136 us (5%)
  matrix products  120 us (4%)
  starting transfers between devices  61.4 us (2%)
    unnamed x3, blocking collectives  665 us
    all_gather x1, waiting for transfers between devices, shards(): lax.all_gather(up_weight, ('seq', 'cp'), axis=0, tiled=True)  323 us
    all_gather x1, waiting for transfers between devices, shards(): lax.all_gather(down_weight, ('seq', 'cp'), axis=0, tiled=True)  290 us
    all_gather x1, blocking collectives, shards(): lax.all_gather(key_weight, ('seq', 'cp'), axis=0, tiled=True)  280 us
    all_gather x1, blocking collectives, shards(): lax.all_gather(value_weight, ('seq', 'cp'), axis=0, tiled=True)  279 us
    all_gather x1, waiting for transfers between devices, shards(): lax.all_gather(gate_weight, ('seq', 'cp'), axis=0, tiled=True)  242 us
    unnamed x29, waiting for transfers between devices  193 us
    unnamed x216, local copies, waits for them, and re-layouts  126 us
  transfers between devices with their start and end apart: 28, of which 15 were waited for; matrix products, arithmetic and copies ran while one was open for 25% of the time, Pallas kernels for 0%

commit v1 on v0

v1 whole, which is shorter than its diff:
```python
import jax
import jax.numpy as jnp
import numpy as np
from jax import lax
from jax.sharding import Mesh
from jax.sharding import PartitionSpec as P

NY, NXH, NC, NXL, NZ = 4, 2, 2, 2, 4
NX = NXH * NXL
AXES = ("y", "xh", "c", "xl", "z")
SEQ = ("y", "xh", "c")
CP = ("xl", "z")
XZ = ("xh", "xl", "z")
YC = ("y", "c")
D, FF, HQ, HD = 1152, 6912, 4, 256
TOK, LEN = 128, 1024
PART = FF // 8
OWN, PAD = 54, 56
WIDE = 16 * PAD
EPS = 1e-6
f32, bf16 = jnp.float32, jnp.bfloat16


def dot(a, b):
    return lax.dot_general(a, b, (((1,), (0,)), ((), ())), preferred_element_type=f32)


def dot_nt(a, b):
    return lax.dot_general(a, b, (((1,), (1,)), ((), ())), preferred_element_type=f32)


def dot_tn(a, b):
    return lax.dot_general(a, b, (((0,), (0,)), ((), ())), preferred_element_type=f32)


def split_dot_nt(a, b):
    high = a.astype(bf16)
    low = (a - high.astype(f32)).astype(bf16)
    return dot_nt(high, b) + dot_nt(low, b)


def swap(x):
    return lax.ppermute(x, "c", [(0, 1), (1, 0)])


def spread(x, axis, count):
    copies = jnp.broadcast_to(x[None], (count,) + x.shape)
    return lax.all_to_all(copies, axis, 0, 0, tiled=True)


def collect(x, axis, count):
    parts = x.reshape((count, x.shape[0] // count) + x.shape[1:])
    parts = lax.all_to_all(parts, axis, 0, 0, tiled=True)
    return jnp.sum(parts.astype(f32), axis=0)


def inverse_rms(u):
    return lax.rsqrt(jnp.mean(u * u, axis=-1, keepdims=True) + EPS)


def norm_back(dy, u, r, w):
    n = u * r
    dn = dy * w
    du = r * (dn - n * jnp.mean(dn * n, axis=-1, keepdims=True))
    return du, dy * n


def one_hot(position, width):
    return (position[:, None] == jnp.arange(width, dtype=jnp.int32)[None, :]).astype(bf16)


def owner_parts(owner):
    z = owner % NZ
    xl = (owner // NZ) % NXL
    c = (owner // (NZ * NXL)) % NC
    xh = (owner // (NZ * NXL * NC)) % NXH
    y = owner // (NZ * NXL * NC * NXH)
    return y, xh, c, xl, z


def mixer_order(rows, core):
    n = jnp.arange(128 * rows, dtype=jnp.int32)
    y, xh, c, xl, z = owner_parts(n // rows)
    half = jnp.where(c == core, 0, 1)
    return ((((half * NY + y) * NXH + xh) * NXL + xl) * NZ + z) * 9 + n % rows


def feed_order():
    n = np.arange(D)
    y, xh, c, xl, z = owner_parts(n // 9)
    return jnp.asarray((((xh * NXL + xl) * NZ + z) * 8 + y * NC + c) * 9 + n % 9, jnp.int32)


def rope_tables(cp_index):
    h = TOK // 2
    rows = np.arange(LEN)
    owner, inside = rows // TOK, rows % TOK
    block = np.where(inside < h, owner, LEN // h - 1 - owner)
    places = (block * h + inside % h).astype(np.int32)
    frequency = (1000000.0 ** (-(np.arange(HD // 2, dtype=np.float32) * 2.0 / HD))).astype(np.float32)
    angles = places.astype(np.float32)[:, None] * frequency[None, :]
    cosine, sine = np.cos(angles).astype(np.float32), np.sin(angles).astype(np.float32)

    def own(table):
        return lax.dynamic_slice_in_dim(jnp.asarray(table), cp_index * TOK, TOK, 0)

    return own(places), jnp.asarray(places), own(cosine), own(sine)


def rope(v, cosine, sine):
    a, b = v[..., : HD // 2], v[..., HD // 2 :]
    return jnp.concatenate([a * cosine - b * sine, b * cosine + a * sine], axis=-1)


def rope_back(g, cosine, sine):
    a, b = g[..., : HD // 2], g[..., HD // 2 :]
    return jnp.concatenate([a * cosine + b * sine, b * cosine - a * sine], axis=-1)


def ring_sum(x, axis, count, index):
    block = x.shape[0] // count
    total = lax.dynamic_slice_in_dim(x, index * block, block, 0).astype(f32)
    for step in (1, count - 1, 2):
        target = lax.rem(index + step, count)
        piece = lax.dynamic_slice_in_dim(x, target * block, block, 0)
        pairs = [(i, (i + step) % count) for i in range(count)]
        total = total + lax.ppermute(piece, axis, pairs).astype(f32)
    return total


def shards(
    hidden,
    lengths,
    entry_gain,
    query_weight,
    key_weight,
    value_weight,
    query_gain,
    key_gain,
    output_weight,
    mixer_gain,
    feed_gain,
    gate_weight,
    up_weight,
    down_weight,
    closing_gain,
    cotangent,
):
    core = lax.axis_index("c")
    x_index = lax.axis_index(("xh", "xl"))
    z_index = lax.axis_index("z")
    cp_index = lax.axis_index(CP)
    places_own, places_all, cosine, sine = rope_tables(cp_index)
    stream = hidden[0].astype(f32)
    upstream = cotangent[0].astype(f32)

    def columns(w):
        parts = w.reshape(9, NY, NXH, NC, PART // 2)
        return parts.transpose(1, 3, 0, 2, 4).reshape(8, 9, PART)

    to_wide = one_hot((jnp.arange(PART, dtype=jnp.int32) // OWN) * PAD + jnp.arange(PART, dtype=jnp.int32) % OWN, WIDE)
    gate_up = jnp.concatenate([columns(gate_weight), columns(up_weight)], axis=2)
    gate_up = lax.all_to_all(gate_up, YC, 0, 0, tiled=True).reshape(72, 2 * PART)
    gate_up = jnp.concatenate(
        [dot(gate_up[:, :PART], to_wide).astype(bf16), dot(gate_up[:, PART:], to_wide).astype(bf16)], axis=1
    )
    down = jnp.pad(down_weight, ((0, PAD - OWN), (0, 2 * WIDE - D)))
    feed_all = lax.all_gather(jnp.concatenate([gate_up, down], axis=0), XZ, axis=0, tiled=False)

    gains = [entry_gain, mixer_gain, feed_gain, closing_gain]
    gains += [jnp.pad(query_gain, (0, 7)), jnp.pad(key_gain, (0, 7))]
    gains = jnp.pad(jnp.stack(gains, axis=1), ((0, 0), (0, 122)))
    mixer_rows = jnp.concatenate(
        [query_weight, key_weight, value_weight, jnp.pad(output_weight, ((0, 1), (0, 0))), gains], axis=1
    )
    mixer_rows = spread(mixer_rows, XZ, 16).reshape(144, 2816)
    own_half = spread(mixer_rows, "y", NY).reshape(576, 2816)
    other_half = swap(own_half)
    project_own, project_other = own_half[:, :1536], other_half[:, :1536]
    output_own, output_other = own_half[:, 1536:2688], other_half[:, 1536:2688]

    to_mixer = one_hot(mixer_order(9, core), D)
    to_output = one_hot(mixer_order(8, core), D)
    to_feed = one_hot(feed_order(), D)
    gains = jnp.concatenate([own_half[:, 2688:], other_half[:, 2688:]], axis=0)
    gains = lax.dot_general(gains, to_mixer, (((0,), (1,)), ((), ())), preferred_element_type=f32)
    entry_scale, mixer_scale, feed_scale, closing_scale = (gains[i : i + 1] for i in range(4))
    query_scale, key_scale = gains[4:6].reshape(2, 128, 9)[:, :, :2].reshape(2, HD)

    entry_r = inverse_rms(stream)
    entry_in = dot((stream * entry_r * entry_scale).astype(bf16), to_mixer).astype(bf16)
    raw = dot(entry_in[:, :576], project_own) + dot(entry_in[:, 576:], project_other)
    query_raw = raw[:, : HQ * HD].reshape(TOK, HQ, HD).transpose(1, 0, 2)
    key_raw, value_raw = raw[:, HQ * HD : HQ * HD + HD], raw[:, HQ * HD + HD :]
    query_r, key_r = inverse_rms(query_raw), inverse_rms(key_raw)
    query_low = (rope(query_raw * query_r * query_scale, cosine, sine) * HD**-0.5).astype(bf16)
    query_low = query_low.reshape(HQ * TOK, HD)
    key_low = rope(key_raw * key_r * key_scale, cosine, sine).astype(bf16)
    couple = spread(jnp.concatenate([key_low, value_raw.astype(bf16)], axis=1), CP, 8).reshape(LEN, 2 * HD)
    key_all, value_all = couple[:, :HD], couple[:, HD:]
    allowed = (places_all[None, :] <= places_own[:, None]) & (places_all[None, :] < lengths[0])
    scores = dot_nt(query_low, key_all).reshape(HQ, TOK, LEN)
    scores = jnp.where(allowed[None], scores, -1e30)
    soft = jax.nn.softmax(scores, axis=-1).reshape(HQ * TOK, LEN)
    soft_low = soft.astype(bf16)
    mixed = dot(soft_low, value_all).astype(bf16).reshape(HQ, TOK, HD).transpose(1, 0, 2).reshape(TOK, HQ * HD)
    mixed = dot(mixed, to_output).astype(bf16)
    mixer_out = dot(mixed[:, :576], output_own) + dot(mixed[:, 576:], output_other)
    mixer_r = inverse_rms(mixer_out)
    middle = stream + mixer_out * mixer_r * mixer_scale

    gate_up = feed_all[:, :72].reshape(D, 2 * WIDE)
    down = feed_all[:, 72:, :D].reshape(WIDE, D)

    def gather_tokens(x):
        own = spread(x, "y", NY).reshape(NY * TOK, D)
        return jnp.concatenate([own, swap(own)], axis=0)

    def sum_tokens(x):
        own = x[: NY * TOK] + swap(x[NY * TOK :].astype(bf16)).astype(f32)
        return collect(own.astype(bf16), "y", NY)

    feed_r = inverse_rms(middle)
    feed_in = dot((middle * feed_r * feed_scale).astype(bf16), to_feed).astype(bf16)
    feed_in = gather_tokens(feed_in)
    gate_out = dot(feed_in, gate_up[:, :WIDE])
    up_out = dot(feed_in, gate_up[:, WIDE:])
    product = (jax.nn.gelu(gate_out, approximate=True) * up_out).astype(bf16)
    down_out = sum_tokens(dot(product, down))
    down_r = inverse_rms(down_out)
    layer_output = (middle + down_out * down_r * closing_scale).astype(bf16)

    down_grad, closing_part = norm_back(upstream, down_out, down_r, closing_scale)
    down_grad = gather_tokens(down_grad.astype(bf16))
    product_grad = dot_nt(down_grad, down)
    down_delta = dot_tn(product, down_grad).astype(bf16)
    _, gated_pull = jax.vjp(lambda g, u: jax.nn.gelu(g, approximate=True) * u, gate_out, up_out)
    gate_grad, up_grad = gated_pull(product_grad)
    gate_up_grad = jnp.concatenate([gate_grad.astype(bf16), up_grad.astype(bf16)], axis=1)
    feed_in_grad = sum_tokens(dot_nt(gate_up_grad, gate_up))
    gate_up_delta = dot_tn(feed_in, gate_up_grad).astype(bf16)

    down_share = ring_sum(down_delta, ("xh", "xl"), NX, x_index).astype(bf16)
    down_share = ring_sum(down_share, "z", NZ, z_index)[:OWN]
    gate_up_share = ring_sum(gate_up_delta, ("xh", "xl"), NX, x_index).astype(bf16)
    gate_up_share = ring_sum(gate_up_share, "z", NZ, z_index).astype(bf16)
    gate_up_share = jnp.concatenate(
        [dot_nt(gate_up_share[:, :WIDE], to_wide), dot_nt(gate_up_share[:, WIDE:], to_wide)], axis=1
    ).astype(bf16)
    gate_up_share = lax.all_to_all(gate_up_share.reshape(8, 9, 2 * PART), YC, 0, 0, tiled=True).astype(f32)

    def rows(share):
        return share.reshape(NY, NC, 9, NXH, PART // 2).transpose(2, 0, 3, 1, 4).reshape(9, FF)

    gate_delta, upward_delta = rows(gate_up_share[:, :, :PART]), rows(gate_up_share[:, :, PART:])

    feed_in_grad = split_dot_nt(feed_in_grad, to_feed)
    middle_part, feed_part = norm_back(feed_in_grad, middle, feed_r, feed_scale)
    middle_grad = upstream + middle_part
    mixer_out_grad, mixer_part = norm_back(middle_grad, mixer_out, mixer_r, mixer_scale)
    mixer_out_grad = mixer_out_grad.astype(bf16)
    mixed_grad = jnp.concatenate([dot_nt(mixer_out_grad, output_own), dot_nt(mixer_out_grad, output_other)], axis=1)
    mixed_grad = dot_nt(mixed_grad.astype(bf16), to_output).astype(bf16)
    mixed_grad = mixed_grad.reshape(TOK, HQ, HD).transpose(1, 0, 2).reshape(HQ * TOK, HD)
    value_dots = dot_nt(mixed_grad, value_all)
    score_grad = soft * (value_dots - jnp.sum(soft * value_dots, axis=-1, keepdims=True))
    score_grad = score_grad.astype(bf16)
    key_term = dot_tn(score_grad, query_low)
    value_term = dot_tn(soft_low, mixed_grad)
    couple_grad = jnp.concatenate([key_term, value_term], axis=1).astype(bf16)
    couple_grad = collect(couple_grad, CP, 8)
    key_grad, value_grad = couple_grad[:, :HD], couple_grad[:, HD:]
    query_grad = dot(score_grad, key_all).reshape(HQ, TOK, HD)
    query_grad = rope_back(query_grad * HD**-0.5, cosine, sine)
    query_raw_grad, query_part = norm_back(query_grad, query_raw, query_r, query_scale)
    key_raw_grad, key_part = norm_back(rope_back(key_grad, cosine, sine), key_raw, key_r, key_scale)
    query_raw_grad = query_raw_grad.astype(bf16).transpose(1, 0, 2).reshape(TOK, HQ * HD)
    raw_grad = jnp.concatenate([query_raw_grad, key_raw_grad.astype(bf16), value_grad.astype(bf16)], axis=1)
    entry_in_grad = jnp.concatenate([dot_nt(raw_grad, project_own), dot_nt(raw_grad, project_other)], axis=1)
    entry_in_grad = split_dot_nt(entry_in_grad, to_mixer)
    stream_part, entry_part = norm_back(entry_in_grad, stream, entry_r, entry_scale)
    hidden_delta = middle_grad + stream_part

    changes = jnp.stack([jnp.sum(t, axis=0) for t in (entry_part, mixer_part, feed_part, closing_part)], axis=0)
    head_changes = jnp.stack([jnp.sum(query_part, axis=(0, 1)), jnp.sum(key_part, axis=0)], axis=0)
    head_changes = jnp.pad(head_changes.reshape(2, 128, 2), ((0, 0), (0, 0), (0, 7))).reshape(2, D)
    changes = jnp.pad(jnp.concatenate([changes, head_changes], axis=0), ((0, 122), (0, 0))).astype(bf16)
    changes = lax.dot_general(to_mixer, changes, (((0,), (1,)), ((), ())), preferred_element_type=f32)
    mixer_delta = jnp.concatenate(
        [dot_tn(entry_in, raw_grad).astype(bf16), dot_tn(mixed, mixer_out_grad).astype(bf16), changes.astype(bf16)],
        axis=1,
    )
    mixer_delta = mixer_delta[:576].astype(f32) + swap(mixer_delta[576:]).astype(f32)
    mixer_delta = collect(mixer_delta.astype(bf16), "y", NY).astype(bf16)
    mixer_delta = collect(mixer_delta, XZ, 16)
    changes = mixer_delta[:, 2688:]

    return (
        layer_output[None],
        hidden_delta[None],
        changes[:, 0],
        mixer_delta[:, :1024],
        mixer_delta[:, 1024:1280],
        mixer_delta[:, 1280:1536],
        changes[:2, 4],
        changes[:2, 5],
        mixer_delta[:8, 1536:2688],
        changes[:, 1],
        changes[:, 2],
        gate_delta,
        upward_delta,
        down_share,
        changes[:, 3],
    )


def solution(mesh):
    chips = Mesh(mesh.devices.reshape(NY, NXH, NC, NXL, NZ), AXES)
    tokens, row, vector = P(SEQ, CP, None), P(AXES, None), P(AXES)
    return jax.shard_map(
        shards,
        mesh=chips,
        in_specs=(
            tokens, P(SEQ), vector, row, row, row, vector, vector,
            row, vector, vector, row, row, row, vector, tokens,
        ),
        out_specs=(
            tokens, tokens, vector, row, row, row, vector, vector,
            row, vector, vector, row, row, row, vector,
        ),
        check_vma=False,
    )
```

time: 2760 us -> 516 us (0.19)
  blocking collectives: 1280 us -> 57.8 us
  waiting for transfers between devices: 1110 us -> 174 us
  local copies, waits for them, and re-layouts: 136 us -> 68.7 us
  matrix products: 120 us -> 80.6 us
    all_gather x5 -> x1, waiting for transfers between devices: 855 us -> 0.02 us  [shards(): lax.all_gather(jnp.concatenate([gate_up, down], axis=0), XZ, axis=0, tile...]
    unnamed x3 -> x0, blocking collectives: 665 us -> none
    all_gather x4 -> x0, blocking collectives: 619 us -> none  [the longest x1 280 us: shards(): lax.all_gather(key_weight, ('seq', 'cp'), axis=0, tiled=True)]
    unnamed x29 -> x1, waiting for transfers between devices: 193 us -> 0.02 us
    all_to_all x0 -> x9, waiting for transfers between devices: none -> 129 us  [the longest x3 67.5 us: spread(): return lax.all_to_all(copies, axis, 0, 0, tiled=True)]
    unnamed x216 -> x180, local copies, waits for them, and re-layouts: 126 us -> 10.6 us
    reduce_scatter x2 -> x0, waiting for transfers between devices: 67.5 us -> none  [the longest x1 37.5 us: shards(): lax.psum_scatter(couple[1].astype(jnp.bfloat16), 'cp', scatter_dimension=...]
    unnamed x21 -> x0, starting transfers between devices: 60.9 us -> none
  transfers between devices with their start and end apart: 28 -> 28, of which waited for: 15 -> 19; matrix products, arithmetic and copies ran while one was open for 25% -> 26% of each run, Pallas kernels for 0% -> 0%
where the time goes in v1:
time: 516 us; the launch traced here: 507 us
  waiting for transfers between devices  174 us (34%)
  matrix products  80.6 us (16%)
  starting transfers between devices  71.1 us (14%)
  local copies, waits for them, and re-layouts  68.7 us (13%)
  blocking collectives  57.8 us (11%)
  other arithmetic  38.2 us (7%)
  between operations  16.9 us (3%)
    all_to_all x3, waiting for transfers between devices, spread(): return lax.all_to_all(copies, axis, 0, 0, tiled=True)  67.5 us
    all_to_all x4, waiting for transfers between devices, collect(): parts = lax.all_to_all(parts, axis, 0, 0, tiled=True)  50.9 us
    all_to_all x2, blocking collectives, spread(): return lax.all_to_all(copies, axis, 0, 0, tiled=True)  37.9 us
    ppermute x12, waiting for transfers between devices, ring_sum(): total = total + lax.ppermute(piece, axis, pairs).astype(f32)  33.2 us
    dot_general x14, matrix products, dot_nt(): lax.dot_general(a, b, (((1,), (1,)), ((), ())), preferred_element_type=f32)  30.1 us
    dot_general x14, matrix products, dot(): lax.dot_general(a, b, (((1,), (0,)), ((), ())), preferred_element_type=f32)  27.1 us
    all_to_all x4, starting transfers between devices, collect(): parts = lax.all_to_all(parts, axis, 0, 0, tiled=True)  22.5 us
    all_to_all x1, blocking collectives, collect(): parts = lax.all_to_all(parts, axis, 0, 0, tiled=True)  19.9 us
  transfers between devices with their start and end apart: 28, of which 19 were waited for; matrix products, arithmetic and copies ran while one was open for 26% of the time, Pallas kernels for 0%

profile of v1, /device:TPU:8, one launch (start us, length us, event | category | flops | bytes accessed | tf_op | source)
XLA Modules:
  0.0 506.9 jit_solution(13437026651007472425)
XLA Ops:
  11.3 4.9 all-to-all-start.4
  16.5 7.9 %all-to-all-done.4 = bf16[8,9,1728]{2,1,0:T(8,128)(2,1)S(1)} async-done(((bf16[8,9,1728]{2,1,0:T(8,128)(2,1)}), bf16[8,9,1728]{2,1,0:T(8,128)(2,1)S(1)}, u32[]{:S(2)}, u32[]{:S(2)}) %all-to-all-start.4) | async-done | bytes 248864 | tf_op jit(solution)/shard_map/all_to_all | solution.py:163
  25.7 7.9 %all-to-all-start = ((bf16[16,9,2816]{2,1,0:T(8,128)(2,1)}), bf16[16,9,2816]{2,1,0:T(8,128)(2,1)S(1)}, u32[]{:S(2)}, u32[]{:S(2)}) async-start(bf16[16,9,2816]{2,1,0:T(8,128)(2,1)} %broadcast_in_dim.35), calls=%async_computation | async-start | bytes 2883584 | tf_op jit(solution)/shard_map/all_to_all | solution.py:48
  35.2 20.4 %all-to-all-done = bf16[16,9,2816]{2,1,0:T(8,128)(2,1)S(1)} async-done(((bf16[16,9,2816]{2,1,0:T(8,128)(2,1)}), bf16[16,9,2816]{2,1,0:T(8,128)(2,1)S(1)}, u32[]{:S(2)}, u32[]{:S(2)}) %all-to-all-start) | async-done | bytes 811040 | tf_op jit(solution)/shard_map/all_to_all | solution.py:48
  56.0 2.0 broadcast_in_dim.37
  58.0 5.3 %all-to-all-start.1 = ((bf16[4,144,2816]{2,1,0:T(8,128)(2,1)}), bf16[4,144,2816]{2,1,0:T(8,128)(2,1)S(1)}, u32[]{:S(2)}, u32[]{:S(2)}) async-start(bf16[4,144,2816]{2,1,0:T(8,128)(2,1)} %broadcast_in_dim.37), calls=%async_computation.1 | async-start | bytes 6488064 | tf_op jit(solution)/shard_map/all_to_all | solution.py:48
  66.8 30.6 %all-to-all-done.1 = bf16[4,144,2816]{2,1,0:T(8,128)(2,1)S(1)} async-done(((bf16[4,144,2816]{2,1,0:T(8,128)(2,1)}), bf16[4,144,2816]{2,1,0:T(8,128)(2,1)S(1)}, u32[]{:S(2)}, u32[]{:S(2)}) %all-to-all-start.1) | async-done | bytes 3244064 | tf_op jit(solution)/shard_map/all_to_all | solution.py:48
  99.9 3.5 collective-permute-done
  111.9 2.0 fusion.38
  114.5 2.1 convolution_add_fusion.1
  119.5 4.7 all-to-all-start.2
  125.3 16.4 %all-to-all-done.2 = bf16[8,128,512]{2,1,0:T(8,128)(2,1)S(1)} async-done(((bf16[8,128,512]{2,1,0:T(8,128)(2,1)}), bf16[8,128,512]{2,1,0:T(8,128)(2,1)S(1)}, u32[]{:S(2)}, u32[]{:S(2)}) %all-to-all-start.2) | async-done | bytes 1048608 | tf_op jit(solution)/shard_map/all_to_all | solution.py:48
  141.7 2.2 fusion.265
  144.0 1.9 broadcast_divide_fusion
  149.7 1.9 multiply_reduce_fusion.6
  153.3 19.3 %all_to_all.60 = bf16[4,128,1152]{2,1,0:T(8,128)(2,1)} all-to-all(bf16[4,128,1152]{2,1,0:T(8,128)(2,1)S(1)} %broadcast_in_dim.40), channel_id=1, replica_groups=mesh['y'=4,'xh'=2,'c'=2,'xl'=2,'z'=4] {'y'}, dimensions={0} | all-to-all | bytes 2359296 | tf_op jit(solution)/shard_map/all_to_all | solution.py:48
  174.6 2.4 slice.268
  177.1 4.3 fusion.49
  181.4 5.2 %multiply_convert_fusion.1 = (bf16[1024,896]{0,1:T(8,128)(2,1)S(1)}, f32[1024,896]{0,1:T(8,128)S(1)}) fusion(f32[1024,896]{0,1:T(8,128)S(1)} %fusion.49, bf16[1152,1792]{1,0:T(8,128)(2,1)S(1)} %bitcast.189, bf16[512,1152]{1,0:T(8,128)(2,1)} %collective-permute-done.1, bf16[512,1152]{1,0:T(8,128)(2,1)} %bitcast.17), kind=kOutput, calls=%fused_computation.30 | convolution fusion | flops 2127822848 | bytes 13598720 | tf_op jit(solution)/shard_map/dot_general | solution.py:25
  186.6 2.9 fusion.270
  190.2 2.5 collective-permute-done.2
  192.9 19.9 %all_to_all.61 = bf16[4,128,1152]{2,1,0:T(8,128)(2,1)S(1)} all-to-all(bf16[4,128,1152]{2,1,0:T(8,128)(2,1)S(1)} %bitcast.187), channel_id=1, replica_groups=mesh['y'=4,'xh'=2,'c'=2,'xl'=2,'z'=4] {'y'}, dimensions={0} | all-to-all | bytes 2359296 | tf_op jit(solution)/shard_map/all_to_all | solution.py:53
  214.4 18.6 %all_to_all.62 = bf16[4,128,1152]{2,1,0:T(8,128)(2,1)S(1)} all-to-all(bf16[4,128,1152]{2,1,0:T(8,128)(2,1)S(1)} %broadcast_in_dim.47), channel_id=1, replica_groups=mesh['y'=4,'xh'=2,'c'=2,'xl'=2,'z'=4] {'y'}, dimensions={0} | all-to-all | bytes 2359296 | tf_op jit(solution)/shard_map/all_to_all | solution.py:48
  233.5 2.8 collective-permute-done.3
  236.3 6.1 %fusion.17 = (bf16[1024,896]{0,1:T(8,128)(2,1)S(1)}, bf16[1024,896]{0,1:T(8,128)(2,1)S(1)}) fusion(f32[1024,896]{0,1:T(8,128)S(1)} %fusion.49, f32[1024,896]{0,1:T(8,128)S(1)} %get-tuple-element.76, bf16[896,1152]{1,0:T(8,128)(2,1)S(1)} %bitcast.197, bf16[512,1152]{1,0:T(8,128)(2,1)S(1)} %collective-permute-done.3, bf16[512,1152]{1,0:T(8,128)(2,1)S(1)} %bitcast.199), kind=kOutput, calls=%fused_computation.27 | convolution fusion | flops 2140667904 | bytes 15433728 | tf_op jit(solution)/shard_map/dot_general | solution.py:29
  242.4 5.0 fusion.40
  247.4 2.1 copy-done.16
  251.5 2.5 collective-permute-done.4
  253.9 3.2 fusion.41
  257.1 5.9 %all-to-all-start.7 = ((bf16[4,128,1152]{2,1,0:T(8,128)(2,1)}), bf16[4,128,1152]{2,1,0:T(8,128)(2,1)}, u32[]{:S(2)}, u32[]{:S(2)}) async-start(bf16[4,128,1152]{2,1,0:T(8,128)(2,1)} %bitcast.186), calls=%async_computation.7 | async-start | bytes 2359296 | tf_op jit(solution)/shard_map/all_to_all | solution.py:53
  263.0 7.3 %convolution_convert_fusion = bf16[1152,1792]{1,0:T(8,128)(2,1)S(1)} fusion(bf16[1024,896]{0,1:T(8,128)(2,1)} %copy-done.86, bf16[1024,896]{0,1:T(8,128)(2,1)} %copy-done.85, bf16[512,1152]{1,0:T(8,128)(2,1)} %collective-permute-done.1, bf16[512,1152]{1,0:T(8,128)(2,1)} %bitcast.17), kind=kOutput, calls=%fused_computation.1 | convolution fusion | flops 4241981440 | bytes 10158080 | tf_op jit(solution)/shard_map/dot_general | solution.py:33
  270.3 2.0 constant_dynamic-slice_fusion.11
  274.8 2.2 collective-permute-start.8
  284.3 1.9 fusion.73
  294.5 4.6 all-to-all-start.8
  300.8 3.5 convolution_convert_fusion.2
  304.3 29.2 %all-to-all-done.8 = bf16[8,128,512]{2,1,0:T(8,128)(2,1)} async-done(((bf16[8,128,512]{2,1,0:T(8,128)(2,1)}), bf16[8,128,512]{2,1,0:T(8,128)(2,1)}, u32[]{:S(2)}, u32[]{:S(2)}) %all-to-all-start.8) | async-done | bytes 1048608 | tf_op jit(solution)/shard_map/all_to_all | solution.py:53
  343.1 2.3 fusion.55
  345.4 2.1 convolution_convert_fusion.1
  352.5 2.2 fusion.52
  354.7 2.0 fusion.5
  356.7 2.8 fusion.106
  361.5 2.1 fusion.34
  364.1 2.0 slice.283
  367.8 2.8 add_convert_fusion.1
  371.9 2.3 collective-permute-start.11
  375.6 3.9 convolution_convert_fusion.3
  380.8 5.5 %collective-permute-done.11 = bf16[72,1792]{1,0:T(8,128)(2,1)S(1)} collective-permute-done((bf16[72,1792]{1,0:T(8,128)(2,1)S(1)}, bf16[72,1792]{1,0:T(8,128)(2,1)S(1)}, u32[]{:S(2)}, u32[]{:S(2)}) %collective-permute-start.11) | collective-permute-done | bytes 258080 | tf_op jit(solution)/shard_map/ppermute | solution.py:127
  389.6 4.8 all-to-all-start.11
  394.5 5.4 %add_convert_fusion = bf16[576,2816]{1,0:T(8,128)(2,1)} fusion(bf16[576,2816]{1,0:T(8,128)(2,1)} %collective-permute-done.5, bf16[1152,2816]{1,0:T(8,128)(2,1)} %copy-done), kind=kLoop, calls=%fused_computation.5 | loop fusion | flops 6488064 | bytes 9732096 | tf_op jit(solution)/shard_map/convert_element_type | solution.py:294
  399.9 2.8 all-to-all-done.11
  403.4 5.1 %all-to-all-start.9 = ((bf16[4,144,2816]{2,1,0:T(8,128)(2,1)}), bf16[4,144,2816]{2,1,0:T(8,128)(2,1)S(1)}, u32[]{:S(2)}, u32[]{:S(2)}) async-start(bf16[4,144,2816]{2,1,0:T(8,128)(2,1)} %bitcast.41), calls=%async_computation.9 | async-start | bytes 6488064 | tf_op jit(solution)/shard_map/all_to_all | solution.py:53
  408.6 2.6 constant_dynamic-slice_fusion.5
  411.1 2.5 collective-permute-start.14
  413.6 2.6 collective-permute-start.13
  416.3 20.5 %collective-permute-done.12 = bf16[224,1152]{1,0:T(8,128)(2,1)} collective-permute-done((bf16[224,1152]{1,0:T(8,128)(2,1)}, bf16[224,1152]{1,0:T(8,128)(2,1)}, u32[]{:S(2)}, u32[]{:S(2)}) %collective-permute-start.12) | collective-permute-done | bytes 516128 | tf_op jit(solution)/shard_map/ppermute | solution.py:127
  441.9 2.8 collective-permute-start.17
  445.2 3.2 collective-permute-done.15
  451.9 2.0 fusion.262
  456.2 2.1 reshape.628
  460.6 2.1 reshape.626
  464.3 2.4 reshape.624
  466.7 6.9 %all-to-all-start.10 = ((bf16[16,9,2816]{2,1,0:T(8,128)(2,1)}), bf16[16,9,2816]{2,1,0:T(8,128)(2,1)S(1)}, u32[]{:S(2)}, u32[]{:S(2)}) async-start(bf16[16,9,2816]{2,1,0:T(8,128)(2,1)} %reshape.624), calls=%async_computation.10 | async-start | bytes 2883584 | tf_op jit(solution)/shard_map/all_to_all | solution.py:53
  474.7 21.2 %all-to-all-done.10 = bf16[16,9,2816]{2,1,0:T(8,128)(2,1)S(1)} async-done(((bf16[16,9,2816]{2,1,0:T(8,128)(2,1)}), bf16[16,9,2816]{2,1,0:T(8,128)(2,1)S(1)}, u32[]{:S(2)}, u32[]{:S(2)}) %all-to-all-start.10) | async-done | bytes 811040 | tf_op jit(solution)/shard_map/all_to_all | solution.py:53
  (341 shorter events, 103.7 us)
Async XLA Ops:
  7.2 9.1 %copy-start.49 = (bf16[9,1024]{1,0:T(8,128)(2,1)S(1)}, bf16[9,1024]{1,0:T(8,128)(2,1)}, u32[]{:S(2)}) copy-start(bf16[9,1024]{1,0:T(8,128)(2,1)} %param.23) | copy-start | bytes 55300
  7.2 9.1 %copy-start.56 = (bf16[9,256]{1,0:T(8,128)(2,1)S(1)}, bf16[9,256]{1,0:T(8,128)(2,1)}, u32[]{:S(2)}) copy-start(bf16[9,256]{1,0:T(8,128)(2,1)} %param.24) | copy-start | bytes 13828
  7.2 9.1 %copy-start.57 = (bf16[9,256]{1,0:T(8,128)(2,1)S(1)}, bf16[9,256]{1,0:T(8,128)(2,1)}, u32[]{:S(2)}) copy-start(bf16[9,256]{1,0:T(8,128)(2,1)} %param.25) | copy-start | bytes 13828
  7.2 9.1 %copy-start.50 = (bf16[8,1152]{1,0:T(8,128)(2,1)S(1)}, bf16[8,1152]{1,0:T(8,128)(2,1)}, u32[]{:S(2)}) copy-start(bf16[8,1152]{1,0:T(8,128)(2,1)} %param.28) | copy-start | bytes 55300
  7.2 9.1 %copy-start.75 = (bf16[2]{0:T(256)(128)(2,1)S(1)}, bf16[2]{0:T(256)(128)(2,1)}, u32[]{:S(2)}) copy-start(bf16[2]{0:T(256)(128)(2,1)} %param.27) | copy-start | bytes 16
  7.2 9.1 %copy-start.76 = (bf16[2]{0:T(256)(128)(2,1)S(1)}, bf16[2]{0:T(256)(128)(2,1)}, u32[]{:S(2)}) copy-start(bf16[2]{0:T(256)(128)(2,1)} %param.26) | copy-start | bytes 16
  7.2 9.1 %copy-start.74 = (bf16[9]{0:T(256)(128)(2,1)S(1)}, bf16[9]{0:T(256)(128)(2,1)}, u32[]{:S(2)}) copy-start(bf16[9]{0:T(256)(128)(2,1)} %param.34) | copy-start | bytes 58
  7.3 9.1 %copy-start.73 = (bf16[9]{0:T(256)(128)(2,1)S(1)}, bf16[9]{0:T(256)(128)(2,1)}, u32[]{:S(2)}) copy-start(bf16[9]{0:T(256)(128)(2,1)} %param.30) | copy-start | bytes 58
  7.3 9.1 %copy-start.72 = (bf16[9]{0:T(256)(128)(2,1)S(1)}, bf16[9]{0:T(256)(128)(2,1)}, u32[]{:S(2)}) copy-start(bf16[9]{0:T(256)(128)(2,1)} %param.29) | copy-start | bytes 58
  7.3 9.1 %copy-start.71 = (bf16[9]{0:T(256)(128)(2,1)S(1)}, bf16[9]{0:T(256)(128)(2,1)}, u32[]{:S(2)}) copy-start(bf16[9]{0:T(256)(128)(2,1)} %param.22) | copy-start | bytes 58
  11.3 13.1 %all-to-all-start.4 = ((bf16[8,9,1728]{2,1,0:T(8,128)(2,1)}), bf16[8,9,1728]{2,1,0:T(8,128)(2,1)S(1)}, u32[]{:S(2)}, u32[]{:S(2)}) async-start(bf16[8,9,1728]{2,1,0:T(8,128)(2,1)} %copy.80), calls=%async_computation.4 | async-start | bytes 917504 | tf_op jit(solution)/shard_map/all_to_all | solution.py:163
  25.7 30.0 %all-to-all-start = ((bf16[16,9,2816]{2,1,0:T(8,128)(2,1)}), bf16[16,9,2816]{2,1,0:T(8,128)(2,1)S(1)}, u32[]{:S(2)}, u32[]{:S(2)}) async-start(bf16[16,9,2816]{2,1,0:T(8,128)(2,1)} %broadcast_in_dim.35), calls=%async_computation | async-start | bytes 2883584 | tf_op jit(solution)/shard_map/all_to_all | solution.py:48
  33.6 29.7 %copy-start.66 = (s32[864]{0:T(1024)}, s32[864]{0:T(1024)S(1)}, u32[]{:S(2)}) copy-start(s32[864]{0:T(1024)S(1)} %fusion.211) | copy-start | bytes 10372
  58.0 40.1 %copy-start.53 = (s32[1024]{0:T(1024)S(1)}, s32[1024]{0:T(1024)}, u32[]{:S(2)}) copy-start(s32[1024]{0:T(1024)} %constant.287.clone) | copy-start | bytes 12292
  58.0 39.4 %all-to-all-start.1 = ((bf16[4,144,2816]{2,1,0:T(8,128)(2,1)}), bf16[4,144,2816]{2,1,0:T(8,128)(2,1)S(1)}, u32[]{:S(2)}, u32[]{:S(2)}) async-start(bf16[4,144,2816]{2,1,0:T(8,128)(2,1)} %broadcast_in_dim.37), calls=%async_computation.1 | async-start | bytes 6488064 | tf_op jit(solution)/shard_map/all_to_all | solution.py:48
  63.3 35.0 %copy-start.12 = (bf16[1,128,1152]{2,1,0:T(8,128)(2,1)S(1)}, bf16[1,128,1152]{2,1,0:T(8,128)(2,1)}, u32[]{:S(2)}) copy-start(bf16[1,128,1152]{2,1,0:T(8,128)(2,1)} %param.20) | copy-start | bytes 884740
  63.3 109.6 %all-gather.3.cloned.1.call-start = ((), (), s32[]{:S(2)}) async-start(), calls=%async_computation.12 | async-start | bytes 7798784 | tf_op jit(solution)/shard_map/all_gather | solution.py:168
  97.5 16.5 %copy-start.1 = (bf16[4,144,2816]{2,1,0:T(8,128)(2,1)}, bf16[4,144,2816]{2,1,0:T(8,128)(2,1)S(1)}, u32[]{:S(2)}) copy-start(bf16[4,144,2816]{2,1,0:T(8,128)(2,1)S(1)} %all-to-all-done.1) | copy-start | bytes 9732100
  97.5 5.9 %collective-permute-start = (bf16[576,2816]{1,0:T(8,128)(2,1)S(1)}, bf16[576,2816]{1,0:T(8,128)(2,1)}, u32[]{:S(2)}, u32[]{:S(2)}) collective-permute-start(bf16[576,2816]{1,0:T(8,128)(2,1)S(1)} %bitcast.178), channel_id=1, source_target_pairs={{0,8},{8,0},{1,9},{9,1},{2,10},{10,2},{3,11},{11,3},{4,12},{12,4},... | collective-permute-start | bytes 9732104 | tf_op jit(solution)/shard_map/ppermute | solution.py:43
  119.5 22.2 %copy-start.42 = (pred[128,1024]{1,0:T(8,128)(4,1)S(1)}, pred[128,1024]{1,0:T(8,128)(4,1)}, u32[]{:S(2)}) copy-start(pred[128,1024]{1,0:T(8,128)(4,1)} %compare_and_fusion) | copy-start | bytes 393220
  119.5 22.2 %all-to-all-start.2 = ((bf16[8,128,512]{2,1,0:T(8,128)(2,1)}), bf16[8,128,512]{2,1,0:T(8,128)(2,1)S(1)}, u32[]{:S(2)}, u32[]{:S(2)}) async-start(bf16[8,128,512]{2,1,0:T(8,128)(2,1)} %broadcast_in_dim.38), calls=%async_computation.2 | async-start | bytes 2097152 | tf_op jit(solution)/shard_map/all_to_all | solution.py:48
  124.3 22.4 %copy-start.64 = (s32[1024]{0:T(1024)}, s32[1024]{0:T(1024)S(1)}, u32[]{:S(2)}) copy-start(s32[1024]{0:T(1024)S(1)} %fusion.224) | copy-start | bytes 12292
  125.3 18.7 %copy-start.37 = (f32[4,128,128]{2,1,0:T(8,128)}, f32[4,128,128]{2,1,0:T(8,128)S(1)}, u32[]{:S(2)}) copy-start(f32[4,128,128]{2,1,0:T(8,128)S(1)} %get-tuple-element.57) | copy-start | bytes 786436
  125.3 18.7 %copy-start.39 = (f32[4,128,128]{2,1,0:T(8,128)}, f32[4,128,128]{2,1,0:T(8,128)S(1)}, u32[]{:S(2)}) copy-start(f32[4,128,128]{2,1,0:T(8,128)S(1)} %get-tuple-element.58) | copy-start | bytes 786436
  151.9 20.7 %copy-start.6 = (f32[128,1152]{1,0:T(8,128)}, f32[128,1152]{1,0:T(8,128)S(1)}, u32[]{:S(2)}) copy-start(f32[128,1152]{1,0:T(8,128)S(1)} %get-tuple-element.39) | copy-start | bytes 1769476
  172.6 4.5 collective-permute-start.1
  189.7 3.0 collective-permute-start.2
  192.9 20.2 %copy-start.7 = (f32[128,1152]{1,0:T(8,128)S(1)}, f32[128,1152]{1,0:T(8,128)}, u32[]{:S(2)}) copy-start(f32[128,1152]{1,0:T(8,128)} %copy-done.6) | copy-start | bytes 1769476
  192.9 20.2 %copy-start.15 = (bf16[1,128,1152]{2,1,0:T(8,128)(2,1)S(1)}, bf16[1,128,1152]{2,1,0:T(8,128)(2,1)}, u32[]{:S(2)}) copy-start(bf16[1,128,1152]{2,1,0:T(8,128)(2,1)} %param.35) | copy-start | bytes 884740
  233.0 9.4 %copy-start.25 = (bf16[4,128,1152]{2,1,0:T(8,128)(2,1)}, bf16[4,128,1152]{2,1,0:T(8,128)(2,1)S(1)}, u32[]{:S(2)}) copy-start(bf16[4,128,1152]{2,1,0:T(8,128)(2,1)S(1)} %all_to_all.62) | copy-start | bytes 3538948
  233.0 3.3 collective-permute-start.3
  250.7 3.2 collective-permute-start.4
  257.1 21.6 %all-to-all-start.7 = ((bf16[4,128,1152]{2,1,0:T(8,128)(2,1)}), bf16[4,128,1152]{2,1,0:T(8,128)(2,1)}, u32[]{:S(2)}, u32[]{:S(2)}) async-start(bf16[4,128,1152]{2,1,0:T(8,128)(2,1)} %bitcast.186), calls=%async_computation.7 | async-start | bytes 2359296 | tf_op jit(solution)/shard_map/all_to_all | solution.py:53
  270.3 10.0 %copy-start.80 = (s32[1152]{0:T(1024)S(1)}, s32[1152]{0:T(1024)}, u32[]{:S(2)}) copy-start(s32[1152]{0:T(1024)} %constant.290.clone) | copy-start | bytes 13828
  273.3 8.3 %copy-start.48 = (f32[1152]{0:T(1024)S(1)}, f32[1152]{0:T(1024)}, u32[]{:S(2)}) copy-start(f32[1152]{0:T(1024)} %get-tuple-element.28) | copy-start | bytes 13828
  273.3 94.5 %collective-permute-start.6 = (bf16[288,1792]{1,0:T(8,128)(2,1)}, bf16[288,1792]{1,0:T(8,128)(2,1)}, u32[]{:S(2)}, u32[]{:S(2)}) collective-permute-start(bf16[288,1792]{1,0:T(8,128)(2,1)} %get-tuple-element.42), channel_id=1, source_target_pairs={{0,4},{4,16},{16,20},{20,0},{1,5},{5,17},{17,21},{21,1},{2,6},{6,1... | collective-permute-start | bytes 3096584 | tf_op jit(solution)/shard_map/ppermute | solution.py:127
  274.8 93.1 %collective-permute-start.8 = (bf16[288,1792]{1,0:T(8,128)(2,1)}, bf16[288,1792]{1,0:T(8,128)(2,1)}, u32[]{:S(2)}, u32[]{:S(2)}) collective-permute-start(bf16[288,1792]{1,0:T(8,128)(2,1)} %get-tuple-element.43), channel_id=1, source_target_pairs={{0,16},{4,20},{16,0},{20,4},{1,17},{5,21},{17,1},{21,5},{2,18},{6,... | collective-permute-start | bytes 3096584 | tf_op jit(solution)/shard_map/ppermute | solution.py:127
  277.0 90.9 %collective-permute-start.7 = (bf16[288,1792]{1,0:T(8,128)(2,1)}, bf16[288,1792]{1,0:T(8,128)(2,1)}, u32[]{:S(2)}, u32[]{:S(2)}) collective-permute-start(bf16[288,1792]{1,0:T(8,128)(2,1)} %get-tuple-element.44), channel_id=1, source_target_pairs={{0,20},{4,0},{16,4},{20,16},{1,21},{5,1},{17,5},{21,17},{2,22},{6,... | collective-permute-start | bytes 3096584 | tf_op jit(solution)/shard_map/ppermute | solution.py:127
  294.5 39.0 %all-to-all-start.8 = ((bf16[8,128,512]{2,1,0:T(8,128)(2,1)}), bf16[8,128,512]{2,1,0:T(8,128)(2,1)}, u32[]{:S(2)}, u32[]{:S(2)}) async-start(bf16[8,128,512]{2,1,0:T(8,128)(2,1)} %pad_maximum_fusion.8), calls=%async_computation.8 | async-start | bytes 2097152 | tf_op jit(solution)/shard_map/all_to_all | solution.py:53
  300.6 38.2 %copy-start.52 = (f32[256]{0:T(256)S(1)}, f32[256]{0:T(256)}, u32[]{:S(2)}) copy-start(f32[256]{0:T(256)} %mul.660) | copy-start | bytes 3076
  300.6 38.2 %copy-start.63 = (f32[128]{0:T(128)S(1)}, f32[128]{0:T(128)}, u32[]{:S(2)}) copy-start(f32[128]{0:T(128)} %copy-done.62) | copy-start | bytes 1540
  300.8 42.3 %copy-start.2 = (bf16[4,144,2816]{2,1,0:T(8,128)(2,1)S(1)}, bf16[4,144,2816]{2,1,0:T(8,128)(2,1)}, u32[]{:S(2)}) copy-start(bf16[4,144,2816]{2,1,0:T(8,128)(2,1)} %copy-done.1) | copy-start | bytes 9732100
  304.3 38.8 %copy-start.27 = (bf16[128,4,256]{0,2,1:T(8,128)(2,1)S(1)}, bf16[128,4,256]{0,2,1:T(8,128)(2,1)}, u32[]{:S(2)}) copy-start(bf16[128,4,256]{0,2,1:T(8,128)(2,1)} %copy.82) | copy-start | bytes 786436
  367.8 26.7 %collective-permute-start.5 = (bf16[576,2816]{1,0:T(8,128)(2,1)}, bf16[576,2816]{1,0:T(8,128)(2,1)}, u32[]{:S(2)}, u32[]{:S(2)}) collective-permute-start(bf16[576,2816]{1,0:T(8,128)(2,1)} %slice.283), channel_id=1, source_target_pairs={{0,8},{8,0},{1,9},{9,1},{2,10},{10,2},{3,11},{11,3},{4,12},{12,4},... | collective-permute-start | bytes 9732104 | tf_op jit(solution)/shard_map/ppermute | solution.py:43
  367.8 7.8 %copy-start.78 = (bf16[512,1152]{1,0:T(8,128)(2,1)S(1)}, bf16[512,1152]{1,0:T(8,128)(2,1)}, u32[]{:S(2)}) copy-start(bf16[512,1152]{1,0:T(8,128)(2,1)} %copy-done.77) | copy-start | bytes 3538948
  367.8 7.8 %copy-start.84 = (bf16[1024,896]{0,1:T(8,128)(2,1)S(1)}, bf16[1024,896]{0,1:T(8,128)(2,1)}, u32[]{:S(2)}) copy-start(bf16[1024,896]{0,1:T(8,128)(2,1)} %copy-done.83) | copy-start | bytes 5505028
  370.7 10.1 %collective-permute-start.9 = (bf16[72,1792]{1,0:T(8,128)(2,1)S(1)}, bf16[72,1792]{1,0:T(8,128)(2,1)S(1)}, u32[]{:S(2)}, u32[]{:S(2)}) collective-permute-start(bf16[72,1792]{1,0:T(8,128)(2,1)S(1)} %get-tuple-element.52), channel_id=1, source_target_pairs={{0,1},{1,2},{2,3},{3,0},{4,5},{5,6},{6,7},{7,4},{8,9},{9,10},{10,1... | collective-permute-start | bytes 774152 | tf_op jit(solution)/shard_map/ppermute | solution.py:127
  371.9 14.4 %collective-permute-start.11 = (bf16[72,1792]{1,0:T(8,128)(2,1)S(1)}, bf16[72,1792]{1,0:T(8,128)(2,1)S(1)}, u32[]{:S(2)}, u32[]{:S(2)}) collective-permute-start(bf16[72,1792]{1,0:T(8,128)(2,1)S(1)} %get-tuple-element.53), channel_id=1, source_target_pairs={{0,2},{1,3},{2,0},{3,1},{4,6},{5,7},{6,4},{7,5},{8,10},{9,11},{10,... | collective-permute-start | bytes 774152 | tf_op jit(solution)/shard_map/ppermute | solution.py:127
  374.2 12.7 %copy-start.67 = (s32[864]{0:T(1024)S(1)}, s32[864]{0:T(1024)}, u32[]{:S(2)}) copy-start(s32[864]{0:T(1024)} %copy-done.66) | copy-start | bytes 10372
  374.2 12.6 %collective-permute-start.10 = (bf16[72,1792]{1,0:T(8,128)(2,1)S(1)}, bf16[72,1792]{1,0:T(8,128)(2,1)S(1)}, u32[]{:S(2)}, u32[]{:S(2)}) collective-permute-start(bf16[72,1792]{1,0:T(8,128)(2,1)S(1)} %get-tuple-element.54), channel_id=1, source_target_pairs={{0,3},{1,0},{2,1},{3,2},{4,7},{5,4},{6,5},{7,6},{8,11},{9,8},{10,9... | collective-permute-start | bytes 774152 | tf_op jit(solution)/shard_map/ppermute | solution.py:127
  389.6 13.0 %all-to-all-start.11 = ((bf16[8,9,1728]{2,1,0:T(8,128)(2,1)}), bf16[8,9,1728]{2,1,0:T(8,128)(2,1)S(1)}, u32[]{:S(2)}, u32[]{:S(2)}) async-start(bf16[8,9,1728]{2,1,0:T(8,128)(2,1)} %pad_maximum_fusion.14), calls=%async_computation.11 | async-start | bytes 917504 | tf_op jit(solution)/shard_map/all_to_all | solution.py:250
  403.4 59.3 %all-to-all-start.9 = ((bf16[4,144,2816]{2,1,0:T(8,128)(2,1)}), bf16[4,144,2816]{2,1,0:T(8,128)(2,1)S(1)}, u32[]{:S(2)}, u32[]{:S(2)}) async-start(bf16[4,144,2816]{2,1,0:T(8,128)(2,1)} %bitcast.41), calls=%async_computation.9 | async-start | bytes 6488064 | tf_op jit(solution)/shard_map/all_to_all | solution.py:53
  411.1 25.6 %collective-permute-start.12 = (bf16[224,1152]{1,0:T(8,128)(2,1)}, bf16[224,1152]{1,0:T(8,128)(2,1)}, u32[]{:S(2)}, u32[]{:S(2)}) collective-permute-start(bf16[224,1152]{1,0:T(8,128)(2,1)} %get-tuple-element.45), channel_id=1, source_target_pairs={{0,4},{4,16},{16,20},{20,0},{1,5},{5,17},{17,21},{21,1},{2,6},{6,1... | collective-permute-start | bytes 1548296 | tf_op jit(solution)/shard_map/ppermute | solution.py:127
  411.1 25.6 %collective-permute-start.14 = (bf16[224,1152]{1,0:T(8,128)(2,1)}, bf16[224,1152]{1,0:T(8,128)(2,1)}, u32[]{:S(2)}, u32[]{:S(2)}) collective-permute-start(bf16[224,1152]{1,0:T(8,128)(2,1)} %get-tuple-element.46), channel_id=1, source_target_pairs={{0,16},{4,20},{16,0},{20,4},{1,17},{5,21},{17,1},{21,5},{2,18},{6,... | collective-permute-start | bytes 1548296 | tf_op jit(solution)/shard_map/ppermute | solution.py:127
  413.6 23.7 %collective-permute-start.13 = (bf16[224,1152]{1,0:T(8,128)(2,1)}, bf16[224,1152]{1,0:T(8,128)(2,1)}, u32[]{:S(2)}, u32[]{:S(2)}) collective-permute-start(bf16[224,1152]{1,0:T(8,128)(2,1)} %get-tuple-element.47), channel_id=1, source_target_pairs={{0,20},{4,0},{16,4},{20,16},{1,21},{5,1},{17,5},{21,17},{2,22},{6,... | collective-permute-start | bytes 1548296 | tf_op jit(solution)/shard_map/ppermute | solution.py:127
  440.6 7.7 %collective-permute-start.15 = (bf16[56,1152]{1,0:T(8,128)(2,1)}, bf16[56,1152]{1,0:T(8,128)(2,1)S(1)}, u32[]{:S(2)}, u32[]{:S(2)}) collective-permute-start(bf16[56,1152]{1,0:T(8,128)(2,1)} %get-tuple-element.62), channel_id=1, source_target_pairs={{0,1},{1,2},{2,3},{3,0},{4,5},{5,6},{6,7},{7,4},{8,9},{9,10},{10,1... | collective-permute-start | bytes 387080 | tf_op jit(solution)/shard_map/ppermute | solution.py:127
  441.9 8.2 %collective-permute-start.17 = (bf16[56,1152]{1,0:T(8,128)(2,1)}, bf16[56,1152]{1,0:T(8,128)(2,1)}, u32[]{:S(2)}, u32[]{:S(2)}) collective-permute-start(bf16[56,1152]{1,0:T(8,128)(2,1)} %get-tuple-element.63), channel_id=1, source_target_pairs={{0,2},{1,3},{2,0},{3,1},{4,6},{5,7},{6,4},{7,5},{8,10},{9,11},{10,... | collective-permute-start | bytes 387080 | tf_op jit(solution)/shard_map/ppermute | solution.py:127
  444.7 5.4 %collective-permute-start.16 = (bf16[56,1152]{1,0:T(8,128)(2,1)S(1)}, bf16[56,1152]{1,0:T(8,128)(2,1)}, u32[]{:S(2)}, u32[]{:S(2)}) collective-permute-start(bf16[56,1152]{1,0:T(8,128)(2,1)S(1)} %get-tuple-element.64), channel_id=1, source_target_pairs={{0,3},{1,0},{2,1},{3,2},{4,7},{5,4},{6,5},{7,6},{8,11},{9,8},{10,9... | collective-permute-start | bytes 387080 | tf_op jit(solution)/shard_map/ppermute | solution.py:127
  464.3 9.4 %copy-start.81 = (f32[128]{0:T(128)S(1)}, f32[128]{0:T(128)}, u32[]{:S(2)}) copy-start(f32[128]{0:T(128)} %get-tuple-element.26) | copy-start | bytes 1540
  464.3 9.4 %copy-start.5 = (f32[128,1152]{1,0:T(8,128)S(1)}, f32[128,1152]{1,0:T(8,128)}, u32[]{:S(2)}) copy-start(f32[128,1152]{1,0:T(8,128)} %copy-done.4) | copy-start | bytes 1769476
  464.3 9.4 %copy-start.14 = (bf16[1,128,1152]{2,1,0:T(8,128)(2,1)S(1)}, bf16[1,128,1152]{2,1,0:T(8,128)(2,1)}, u32[]{:S(2)}) copy-start(bf16[1,128,1152]{2,1,0:T(8,128)(2,1)} %param.20) | copy-start | bytes 884740
  464.3 9.4 %copy-start.29 = (f32[128,1152]{1,0:T(8,128)S(1)}, f32[128,1152]{1,0:T(8,128)}, u32[]{:S(2)}) copy-start(f32[128,1152]{1,0:T(8,128)} %get-tuple-element.80) | copy-start | bytes 1769476
  464.3 9.4 %copy-start.70 = (f32[128]{0:T(128)S(1)}, f32[128]{0:T(128)}, u32[]{:S(2)}) copy-start(f32[128]{0:T(128)} %add_rsqrt_fusion.5) | copy-start | bytes 1540
  466.7 29.2 %all-to-all-start.10 = ((bf16[16,9,2816]{2,1,0:T(8,128)(2,1)}), bf16[16,9,2816]{2,1,0:T(8,128)(2,1)S(1)}, u32[]{:S(2)}, u32[]{:S(2)}) async-start(bf16[16,9,2816]{2,1,0:T(8,128)(2,1)} %reshape.624), calls=%async_computation.10 | async-start | bytes 2883584 | tf_op jit(solution)/shard_map/all_to_all | solution.py:53
  (51 other events, 169.2 us)
Sparse Core Ops, SparseCore 0:
  67.0 74.8 all-gather.2
